TPU v7x, 128 devices: a whole 4x4x4 slice. The times are simulated.
128 devices in a mesh: ens: 8 (over x, y_hi), space: 16 (over y_lo, z, core).
Axes of the slice: x: 4, y: 4 (y_hi: 2, y_lo: 2; y = y_hi * 2 + y_lo), z: 4, core: 2. Of those that a mesh axis runs over, the one named last changes fastest.
Arguments:
- states: bfloat16 [16, 8192, 1024], P('ens', 'space'), may hold values from -6 to 6
- member_noise: float32 [16, 1024], P('ens')
- w_query: bfloat16 [1024, 1024], replicated, may hold values from -1 to 1
- w_key: bfloat16 [1024, 1024], replicated, may hold values from -1 to 1
- w_value: bfloat16 [1024, 1024], replicated, may hold values from -0.1875 to 0.1875
- w_out: bfloat16 [1024, 1024], replicated, may hold values from -0.1875 to 0.1875
- w_decode: bfloat16 [1024, 128], replicated, may hold values from -0.1875 to 0.1875
- target: float32 [8192, 128], P('space')
Outputs:
- state_grad: bfloat16 [16, 8192, 1024], P('ens', 'space')
- loss: float32 [], replicated
All inputs are finite; a program needn't handle non-finite values.
Results may differ from a plain program's by a relative error of at most 0.014.
Values may be sent and summed in bfloat16 or wider, within the bound.
No kernel may reach another device: no remote copies, remote signals or barrier semaphores. Data moves between devices by JAX's collectives and lax.ppermute only.
A program may use at most 192 MiB of HBM per device.

v0:
```python
import math

import jax
import jax.numpy as jnp
from jax import lax
from jax.sharding import PartitionSpec as P

HEADS = 16
WIN = 256


SMOOTH = 0.25


def padded(array, sides, width):
    for axis, dim in sides:
        devices, length = (lax.axis_size(axis), array.shape[dim])
        up = [(i, (i + 1) % devices) for i in range(devices - 1)]
        down = [(j, i) for i, j in up]
        last = lax.slice_in_dim(array, length - width, length, axis=dim)
        initial = lax.slice_in_dim(array, 0, width, axis=dim)
        before = lax.ppermute(last, axis, up)
        after = lax.ppermute(initial, axis, down)
        array = jnp.concatenate([before, array, after], axis=dim)
    return array


def slope(delta):
    return delta * lax.rsqrt(delta * delta + SMOOTH * SMOOTH)


def spread_of(delta):
    return jnp.sqrt(delta * delta + SMOOTH * SMOOTH)


def project(source, weight):
    return jnp.einsum("mrd,de->mre", source, weight, preferred_element_type=jnp.float32).astype(
        jnp.bfloat16
    )


def attend(query_block, keys, values, start, total):
    row_count, width = query_block.shape
    block = min(512, row_count)
    count = row_count // block
    depth = width // HEADS

    def one_block(index):
        first = index * block
        query_piece = query_block.reshape(block, HEADS, depth)
        key_piece = keys.reshape(block + 2 * WIN, HEADS, depth)
        value_piece = values.reshape(block + 2 * WIN, HEADS, depth)
        scores = jnp.einsum(
            "qhd,khd->hqk", query_piece, key_piece, preferred_element_type=jnp.float32
        ) / math.sqrt(depth)
        query_pos = start + first + jnp.arange(block, dtype=jnp.int32)
        key_pos = start + first - WIN + jnp.arange(block + 2 * WIN, dtype=jnp.int32)
        near = (
            (jnp.abs(query_pos[:, None] - key_pos[None, :]) <= WIN)
            & (key_pos[None, :] >= 0)
            & (key_pos[None, :] < total)
        )
        scores = jnp.where(near[None], scores, -1e30)
        top = jnp.max(scores, axis=-1, keepdims=True)
        expo = jnp.exp(scores - top)
        weights = (expo / jnp.sum(expo, axis=-1, keepdims=True)).astype(jnp.bfloat16)
        mixed = jnp.einsum("hqk,khd->qhd", weights, value_piece, preferred_element_type=jnp.float32)
        return mixed.astype(jnp.bfloat16).reshape(block, width)

    return lax.map(one_block, jnp.arange(count, dtype=jnp.int32)).reshape(row_count, width)


def pairwise_member_terms(predict_single, member_group, observed_rows, member_states):
    self_term = predict_single.astype(jnp.float32)
    miss = self_term - observed_rows
    differ = self_term[None] - member_group.astype(jnp.float32)
    loss_gradient = slope(miss) - jnp.sum(slope(differ), axis=0) / (member_states - 1)
    local = jnp.sum(spread_of(miss)) - jnp.sum(spread_of(differ)) / (2 * (member_states - 1))
    return (loss_gradient.astype(jnp.bfloat16), local)


def body(states, member_noise, w_query, w_key, w_value, w_out, w_decode, target):
    member_local, row_count, width = states.shape
    member_states = member_local * lax.axis_size("ens")
    total = row_count * lax.axis_size("space")
    start = lax.axis_index("space") * row_count
    hidden_state = states.astype(jnp.float32) + member_noise[:, None, :]
    normalized_state = (
        hidden_state
        * lax.rsqrt(jnp.mean(hidden_state * hidden_state, axis=-1, keepdims=True) + 1e-05)
    ).astype(jnp.bfloat16)
    query_block = project(normalized_state, w_query)
    stacked = jnp.stack([project(normalized_state, w_key), project(normalized_state, w_value)])
    widened = padded(stacked, (("space", 2),), WIN)
    window_keys = widened[0]
    window_values = widened[1]

    def step_forward(items):
        hid, qry, key_rows, value_rows = items
        mixed = attend(qry, key_rows, value_rows, start, total)
        updated = (hid + jnp.dot(mixed, w_out, preferred_element_type=jnp.float32)).astype(
            jnp.bfloat16
        )
        return jnp.dot(updated, w_decode, preferred_element_type=jnp.float32).astype(jnp.bfloat16)

    predict_states = lax.map(step_forward, (hidden_state, query_block, window_keys, window_values))
    member_group = lax.all_gather(predict_states, "ens", axis=0, tiled=True)

    def total_fair_score(one):
        return pairwise_member_terms(one, member_group, target, member_states)

    loss_gradient, local_score_terms = lax.map(total_fair_score, predict_states)
    loss = lax.psum(jnp.sum(local_score_terms), ("ens", "space")) / (
        member_states * total * w_decode.shape[1]
    )
    state_grad = jnp.einsum(
        "mrv,dv->mrd", loss_gradient, w_decode, preferred_element_type=jnp.float32
    ).astype(jnp.bfloat16)
    return (state_grad, loss)


def solution(mesh):
    in_specs = (P("ens", "space", None), P("ens", None), P(), P(), P(), P(), P(), P("space", None))
    out_specs = (P("ens", "space", None), P())
    return jax.shard_map(body, mesh=mesh, in_specs=in_specs, out_specs=out_specs, check_vma=False)
```

profile of v0, /device:TPU:1, one launch (start us, length us, event | category | flops | bytes accessed | tf_op | source)
XLA Modules:
  0.0 314.7 jit_solution(14370316720031260881)
XLA Ops:
  7.2 4.3 %multiply_reduce_fusion.1 = (f32[2,512]{1,0:T(2,128)S(1)}, f32[2,512,1024]{2,1,0:T(8,128)}) fusion(f32[2,1024]{1,0:T(2,128)} %param.13, bf16[2,512,1024]{2,1,0:T(8,128)(2,1)} %param.12), kind=kLoop, calls=%fused_computation.46 | loop fusion | flops 4193280 | bytes 6303744 | tf_op jit(solution)/shard_map/reduce_sum | solution.py:90
  11.6 2.4 convert_bitcast_fusion.1
  14.1 2.4 convert_bitcast_fusion.2
  16.5 2.4 fusion.23
  18.9 0.3 copy-done.8
  19.2 4.9 %collective-permute-start = (bf16[2,2,256,1024]{3,2,1,0:T(8,128)(2,1)}, bf16[2,2,256,1024]{3,2,1,0:T(8,128)(2,1)}, u32[]{:S(2)}, u32[]{:S(2)}) collective-permute-start(bf16[2,2,256,1024]{3,2,1,0:T(8,128)(2,1)} %get-tuple-element.257), channel_id=1, source_target_pairs={{0,1},{1,2},{2,3},{3,4},{4,5},{5,6},{6,7},{7,8},{8,9},{9,10},{10,1... | collective-permute-start | bytes 6291464 | tf_op jit(solution)/shard_map/ppermute | solution.py:22
  24.1 1.9 collective-permute-start.1
  26.1 6.1 %fusion.34 = bf16[2,512,1024]{2,1,0:T(8,128)(2,1)} fusion(bf16[1024,1024]{1,0:T(8,128)(2,1)} %param.14, f32[2,512]{1,0:T(2,128)S(1)} %add_rsqrt_fusion, f32[2,1024]{1,0:T(2,128)S(1)} %copy-done.12, bf16[2,512,1024]{2,1,0:T(8,128)(2,1)} %param.12), kind=kOutput, calls=%fused_computation.58 | convolution fusion | flops 2152726528 | bytes 6303744 | tf_op jit(solution)/shard_map/mrd,de->mre/dot_general | solution.py:37
  32.2 15.2 %collective-permute-done = bf16[2,2,256,1024]{3,2,1,0:T(8,128)(2,1)} collective-permute-done((bf16[2,2,256,1024]{3,2,1,0:T(8,128)(2,1)}, bf16[2,2,256,1024]{3,2,1,0:T(8,128)(2,1)}, u32[]{:S(2)}, u32[]{:S(2)}) %collective-permute-start) | collective-permute-done | bytes 2097184 | tf_op jit(solution)/shard_map/ppermute | solution.py:22
  47.4 4.4 %collective-permute-done.1 = bf16[2,2,256,1024]{3,2,1,0:T(8,128)(2,1)} collective-permute-done((bf16[2,2,256,1024]{3,2,1,0:T(8,128)(2,1)}, bf16[2,2,256,1024]{3,2,1,0:T(8,128)(2,1)}, u32[]{:S(2)}, u32[]{:S(2)}) %collective-permute-start.1) | collective-permute-done | bytes 2097184 | tf_op jit(solution)/shard_map/ppermute | solution.py:23
  51.8 3.4 %pad_maximum_fusion = bf16[2,2,1024,1024]{3,2,1,0:T(8,128)(2,1)S(1)} fusion(bf16[2,2,256,1024]{3,2,1,0:T(8,128)(2,1)} %collective-permute-done.1, bf16[1,2,512,1024]{3,2,1,0:T(8,128)(2,1)S(1)} %copy-done.7, bf16[1,2,512,1024]{3,2,1,0:T(8,128)(2,1)S(1)} %copy-done.9, bf16[2,2,256,1024]{3,2,1,0:T(8,128)(2,1)} %collective-permute-done), kind=kLoop, calls=%fused_computation.40 | loop fusion | flops 33554432 | bytes 16777216 | tf_op jit(solution)/shard_map/concatenate | solution.py:24
  55.2 3.7 %slice_bitcast_fusion = (bf16[2,1024,1024]{2,1,0:T(8,128)(2,1)}, bf16[2,1024,1024]{2,1,0:T(8,128)(2,1)}) fusion(bf16[2,2,1024,1024]{3,2,1,0:T(8,128)(2,1)S(1)} %pad_maximum_fusion), kind=kLoop, calls=%fused_computation.41 | loop fusion | bytes 16777216 | tf_op jit(solution)/shard_map/squeeze | solution.py:95
  58.9 0.7 broadcast.162.clone
  59.6 106.4 %while.29 = (s32[]{:T(128)}, bf16[2,512,128]{2,1,0:T(8,128)(2,1)}, f32[2,512,1024]{2,1,0:T(8,128)}, bf16[2,1024,1024]{2,1,0:T(8,128)(2,1)}, s32[]{:T(128)}, /*in...) while((s32[]{:T(128)}, bf16[2,512,128]{2,1,0:T(8,128)(2,1)}, ...), condition=%wide.region_4.5_spmd, body=%wide.region_1.4_spmd.sunk | while | flops 3410040320 | bytes 112674040 | solution.py:106
  59.6 1.6 fusion.67
  61.2 4.0 %constant_dynamic-slice_fusion.5 = (bf16[1,1024,1024]{2,1,0:T(8,128)(2,1)}, bf16[1,1024,1024]{2,1,0:T(8,128)(2,1)S(1)}) fusion(bf16[2,1024,1024]{2,1,0:T(8,128)(2,1)} %get-tuple-element.404, s32[]{:T(128)} %get-tuple-element.386, bf16[2,1024,1024]{2,1,0:T(8,128)(2,1)} %get-tuple-element.400), kind=kLoop, calls=%fused_computation.23.clone.1 | loop fusion | bytes 8388612 | tf_op jit(solution)/shard_map/while/body/jit(dynamic_index_in_dim)/dynamic_slice | solution.py:106
  65.2 3.9 %copy.24 = bf16[1,1024,1024]{1,2,0:T(8,128)(2,1)} copy(bf16[1,1024,1024]{2,1,0:T(8,128)(2,1)} %get-tuple-element.364) | data formatting | bytes 4194304 | tf_op jit(solution)/shard_map/while/body/jit(dynamic_index_in_dim)/dynamic_slice | solution.py:106
  69.1 1.3 constant_dynamic-slice_fusion.6
  70.4 1.3 copy.23
  71.7 19.0 %fusion.68 = (f32[16,512]{1,0:T(8,128)S(1)}, f32[16,512,1024]{2,1,0:T(8,128)}) fusion(pred[512,1024]{1,0:T(8,128)(4,1)} %fusion.67, bf16[512,16,64]{0,2,1:T(8,128)(2,1)} %bitcast.110, bf16[1024,16,64]{0,2,1:T(8,128)(2,1)} %bitcast.108), kind=kOutput, calls=%fused_computation.62.clone.1 | convolution fusion | flops 1107297280 | bytes 37257216 | tf_op jit(solution)/shard_map/while/body/eval_jaxpr/while/body/eval_jaxpr/sub | solution.py:65
  90.7 2.5 copy.22
  93.2 15.1 %fusion.69 = bf16[16,64,512]{2,1,0:T(8,128)(2,1)} fusion(bf16[1024,16,64]{0,2,1:T(8,128)(2,1)} %bitcast.109, f32[16,512,1024]{2,1,0:T(8,128)} %get-tuple-element.365, f32[16,512]{1,0:T(8,128)S(1)} %get-tuple-element.366), kind=kOutput, calls=%fused_computation.14.clone.1 | convolution fusion | flops 1091043328 | bytes 36732928 | tf_op jit(solution)/shard_map/while/body/eval_jaxpr/while/body/eval_jaxpr/hqk,khd->qhd/dot_general | solution.py:67
  108.3 3.8 %fusion.70 = bf16[2,512,128]{2,1,0:T(8,128)(2,1)S(1)} fusion(bf16[2,512,128]{2,1,0:T(8,128)(2,1)S(1)} %copy-done.3, s32[]{:T(128)} %get-tuple-element.386, bf16[1024,128]{1,0:T(8,128)(2,1)S(1)} %copy-done.11, f32[2,512,1024]{2,1,0:T(8,128)} %get-tuple-element.399, bf16[512,1024]{0,1:T(8,128)(2,1)} %bitcast.111, bf16[1024,1024]{1,0:T(8,128)(2,1)S(1)} %copy-done.14), kind=kOutput, calls=%fused_computation.18.clone.1 | convolution fusion | flops 1209073664 | bytes 5637120 | tf_op jit(solution)/shard_map/while/body/eval_jaxpr/dot_general | solution.py:104
  112.1 0.7 copy-done.4
  112.8 1.6 fusion.67
  114.4 4.0 %constant_dynamic-slice_fusion.5 = (bf16[1,1024,1024]{2,1,0:T(8,128)(2,1)}, bf16[1,1024,1024]{2,1,0:T(8,128)(2,1)S(1)}) fusion(bf16[2,1024,1024]{2,1,0:T(8,128)(2,1)} %get-tuple-element.404, s32[]{:T(128)} %get-tuple-element.386, bf16[2,1024,1024]{2,1,0:T(8,128)(2,1)} %get-tuple-element.400), kind=kLoop, calls=%fused_computation.23.clone.1 | loop fusion | bytes 8388612 | tf_op jit(solution)/shard_map/while/body/jit(dynamic_index_in_dim)/dynamic_slice | solution.py:106
  118.3 3.9 %copy.24 = bf16[1,1024,1024]{1,2,0:T(8,128)(2,1)} copy(bf16[1,1024,1024]{2,1,0:T(8,128)(2,1)} %get-tuple-element.364) | data formatting | bytes 4194304 | tf_op jit(solution)/shard_map/while/body/jit(dynamic_index_in_dim)/dynamic_slice | solution.py:106
  122.3 1.3 constant_dynamic-slice_fusion.6
  123.6 1.3 copy.23
  124.9 19.0 %fusion.68 = (f32[16,512]{1,0:T(8,128)S(1)}, f32[16,512,1024]{2,1,0:T(8,128)}) fusion(pred[512,1024]{1,0:T(8,128)(4,1)} %fusion.67, bf16[512,16,64]{0,2,1:T(8,128)(2,1)} %bitcast.110, bf16[1024,16,64]{0,2,1:T(8,128)(2,1)} %bitcast.108), kind=kOutput, calls=%fused_computation.62.clone.1 | convolution fusion | flops 1107297280 | bytes 37257216 | tf_op jit(solution)/shard_map/while/body/eval_jaxpr/while/body/eval_jaxpr/sub | solution.py:65
  143.8 2.5 copy.22
  146.4 15.1 %fusion.69 = bf16[16,64,512]{2,1,0:T(8,128)(2,1)} fusion(bf16[1024,16,64]{0,2,1:T(8,128)(2,1)} %bitcast.109, f32[16,512,1024]{2,1,0:T(8,128)} %get-tuple-element.365, f32[16,512]{1,0:T(8,128)S(1)} %get-tuple-element.366), kind=kOutput, calls=%fused_computation.14.clone.1 | convolution fusion | flops 1091043328 | bytes 36732928 | tf_op jit(solution)/shard_map/while/body/eval_jaxpr/while/body/eval_jaxpr/hqk,khd->qhd/dot_general | solution.py:67
  161.5 3.8 %fusion.70 = bf16[2,512,128]{2,1,0:T(8,128)(2,1)S(1)} fusion(bf16[2,512,128]{2,1,0:T(8,128)(2,1)S(1)} %copy-done.3, s32[]{:T(128)} %get-tuple-element.386, bf16[1024,128]{1,0:T(8,128)(2,1)S(1)} %copy-done.11, f32[2,512,1024]{2,1,0:T(8,128)} %get-tuple-element.399, bf16[512,1024]{0,1:T(8,128)(2,1)} %bitcast.111, bf16[1024,1024]{1,0:T(8,128)(2,1)S(1)} %copy-done.14), kind=kOutput, calls=%fused_computation.18.clone.1 | convolution fusion | flops 1209073664 | bytes 5637120 | tf_op jit(solution)/shard_map/while/body/eval_jaxpr/dot_general | solution.py:104
  165.2 0.7 copy-done.4
  166.0 55.7 %all-gather.2.cloned.1.call-done = bf16[16,512,128]{2,1,0:T(8,128)(2,1)} async-done(((bf16[2,512,128]{2,1,0:T(8,128)(2,1)}), bf16[16,512,128]{2,1,0:T(8,128)(2,1)}) %all-gather.2.cloned.1.call-update) | async-done | bytes 2097168 | tf_op jit(solution)/shard_map/all_gather | solution.py:107
  221.7 14.9 %while.30 = (s32[]{:T(128)}, bf16[2,512,128]{2,1,0:T(8,128)(2,1)S(1)}, f32[2]{0:T(128)S(1)}, bf16[2,512,128]{2,1,0:T(8,128)(2,1)}, f32[512,128]{1,0:T(8,128)S(1)...) while((s32[]{:T(128)}, bf16[2,512,128]{2,1,0:T(8,128)(2,1)S(1)}, f32[2]{0:T(128)S(1)}, ...), condition=%wide.region_9.10_spmd, body=%wide.region_5.9_spmd.sunk | while | flops 8192002 | bytes 5243049 | solution.py:112
  221.8 1.0 convert_bitcast_fusion.4
  222.8 4.2 %sqrt_reduce_fusion.4 = (f32[]{:T(128)}, f32[512,128]{1,0:T(8,128)S(1)}) fusion(bf16[16,512,128]{2,1,0:T(8,128)(2,1)} %get-tuple-element.429, f32[512,128]{1,0:T(8,128)S(1)} %convert_bitcast_fusion.4), kind=kLoop, calls=%fused_computation.30.clone.1 | loop fusion | flops 7274495 | bytes 2621444 | tf_op jit(solution)/shard_map/while/body/eval_jaxpr/reduce_sum | solution.py:78
  227.6 0.7 sqrt_reduce_fusion.5
  229.0 0.1 dynamic_update_slice.24
  229.1 0.1 fusion.71
  229.2 1.0 convert_bitcast_fusion.4
  230.2 4.2 %sqrt_reduce_fusion.4 = (f32[]{:T(128)}, f32[512,128]{1,0:T(8,128)S(1)}) fusion(bf16[16,512,128]{2,1,0:T(8,128)(2,1)} %get-tuple-element.429, f32[512,128]{1,0:T(8,128)S(1)} %convert_bitcast_fusion.4), kind=kLoop, calls=%fused_computation.30.clone.1 | loop fusion | flops 7274495 | bytes 2621444 | tf_op jit(solution)/shard_map/while/body/eval_jaxpr/reduce_sum | solution.py:78
  235.1 0.7 sqrt_reduce_fusion.5
  236.4 0.1 dynamic_update_slice.24
  236.7 0.6 reduce_sum.59
  237.3 3.0 convolution_convert_fusion
  240.3 65.8 %psum.7 = f32[]{:T(128)} all-reduce(f32[]{:T(128)} %reduce_sum.59), channel_id=1, replica_groups=mesh['ens'=8,'space'=16] {'ens','space'}, use_global_device_ids=true, to_apply=%region_11.12 | all-reduce | flops 1 | bytes 8 | tf_op jit(solution)/shard_map/psum | solution.py:113
  (49 shorter events, 0.3 us)
Async XLA Ops:
  7.2 4.4 %copy-start = (bf16[1024,1024]{1,0:T(8,128)(2,1)S(1)}, bf16[1024,1024]{1,0:T(8,128)(2,1)}, u32[]{:S(2)}) copy-start(bf16[1024,1024]{1,0:T(8,128)(2,1)} %param.16) | copy-start | bytes 6291460
  7.2 4.4 %copy-start.12 = (f32[2,1024]{1,0:T(2,128)S(1)}, f32[2,1024]{1,0:T(2,128)}, u32[]{:S(2)}) copy-start(f32[2,1024]{1,0:T(2,128)} %param.13) | copy-start | bytes 24580
  7.2 214.5 %all-gather.2.cloned.1.call-start = ((), (), s32[]{:S(2)}) async-start(), calls=%async_computation | async-start | bytes 2359296 | tf_op jit(solution)/shard_map/all_gather | solution.py:107
  7.2 4.4 %copy-start.10 = (bf16[2,512,1024]{2,1,0:T(8,128)(2,1)S(1)}, bf16[2,512,1024]{2,1,0:T(8,128)(2,1)}, u32[]{:S(2)}) copy-start(bf16[2,512,1024]{2,1,0:T(8,128)(2,1)} %param.12) | copy-start | bytes 6291460
  11.6 2.4 copy-start.13
  14.0 2.4 copy-start.6
  16.5 2.7 copy-start.8
  19.2 28.2 %collective-permute-start = (bf16[2,2,256,1024]{3,2,1,0:T(8,128)(2,1)}, bf16[2,2,256,1024]{3,2,1,0:T(8,128)(2,1)}, u32[]{:S(2)}, u32[]{:S(2)}) collective-permute-start(bf16[2,2,256,1024]{3,2,1,0:T(8,128)(2,1)} %get-tuple-element.257), channel_id=1, source_target_pairs={{0,1},{1,2},{2,3},{3,4},{4,5},{5,6},{6,7},{7,8},{8,9},{9,10},{10,1... | collective-permute-start | bytes 6291464 | tf_op jit(solution)/shard_map/ppermute | solution.py:22
  24.1 27.7 %collective-permute-start.1 = (bf16[2,2,256,1024]{3,2,1,0:T(8,128)(2,1)}, bf16[2,2,256,1024]{3,2,1,0:T(8,128)(2,1)}, u32[]{:S(2)}, u32[]{:S(2)}) collective-permute-start(bf16[2,2,256,1024]{3,2,1,0:T(8,128)(2,1)} %get-tuple-element.258), channel_id=1, source_target_pairs={{1,0},{2,1},{3,2},{4,3},{5,4},{6,5},{7,6},{8,7},{9,8},{10,9},{11,1... | collective-permute-start | bytes 6291464 | tf_op jit(solution)/shard_map/ppermute | solution.py:23
  26.0 25.7 %copy-start.7 = (bf16[1,2,512,1024]{3,2,1,0:T(8,128)(2,1)S(1)}, bf16[1,2,512,1024]{3,2,1,0:T(8,128)(2,1)}, u32[]{:S(2)}) copy-start(bf16[1,2,512,1024]{3,2,1,0:T(8,128)(2,1)} %copy-done.6) | copy-start | bytes 6291460
  26.0 25.7 %copy-start.9 = (bf16[1,2,512,1024]{3,2,1,0:T(8,128)(2,1)S(1)}, bf16[1,2,512,1024]{3,2,1,0:T(8,128)(2,1)}, u32[]{:S(2)}) copy-start(bf16[1,2,512,1024]{3,2,1,0:T(8,128)(2,1)} %copy-done.8) | copy-start | bytes 6291460
  59.6 162.1 %copy-start.2 = (f32[512,128]{1,0:T(8,128)S(1)}, f32[512,128]{1,0:T(8,128)}, u32[]{:S(2)}) copy-start(f32[512,128]{1,0:T(8,128)} %param.19) | copy-start | bytes 786436
  93.2 15.1 %copy-start.3 = (bf16[2,512,128]{2,1,0:T(8,128)(2,1)S(1)}, bf16[2,512,128]{2,1,0:T(8,128)(2,1)}, u32[]{:S(2)}) copy-start(bf16[2,512,128]{2,1,0:T(8,128)(2,1)} %get-tuple-element.387) | copy-start | bytes 786436 | tf_op jit(solution)/shard_map/while
  93.2 15.1 %copy-start.11 = (bf16[1024,128]{1,0:T(8,128)(2,1)S(1)}, bf16[1024,128]{1,0:T(8,128)(2,1)}, u32[]{:S(2)}) copy-start(bf16[1024,128]{1,0:T(8,128)(2,1)} %get-tuple-element.406) | copy-start | bytes 786436 | tf_op jit(solution)/shard_map/while
  93.2 15.1 %copy-start.14 = (bf16[1024,1024]{1,0:T(8,128)(2,1)S(1)}, bf16[1024,1024]{1,0:T(8,128)(2,1)}, u32[]{:S(2)}) copy-start(bf16[1024,1024]{1,0:T(8,128)(2,1)} %get-tuple-element.405) | copy-start | bytes 6291460 | tf_op jit(solution)/shard_map/while
  112.1 0.7 copy-start.4
  146.4 15.1 %copy-start.3 = (bf16[2,512,128]{2,1,0:T(8,128)(2,1)S(1)}, bf16[2,512,128]{2,1,0:T(8,128)(2,1)}, u32[]{:S(2)}) copy-start(bf16[2,512,128]{2,1,0:T(8,128)(2,1)} %get-tuple-element.387) | copy-start | bytes 786436 | tf_op jit(solution)/shard_map/while
  146.4 15.1 %copy-start.11 = (bf16[1024,128]{1,0:T(8,128)(2,1)S(1)}, bf16[1024,128]{1,0:T(8,128)(2,1)}, u32[]{:S(2)}) copy-start(bf16[1024,128]{1,0:T(8,128)(2,1)} %get-tuple-element.406) | copy-start | bytes 786436 | tf_op jit(solution)/shard_map/while
  146.4 15.1 %copy-start.14 = (bf16[1024,1024]{1,0:T(8,128)(2,1)S(1)}, bf16[1024,1024]{1,0:T(8,128)(2,1)}, u32[]{:S(2)}) copy-start(bf16[1024,1024]{1,0:T(8,128)(2,1)} %get-tuple-element.405) | copy-start | bytes 6291460 | tf_op jit(solution)/shard_map/while
  165.2 0.7 copy-start.4
  221.8 5.8 %copy-start.5 = (bf16[2,512,128]{2,1,0:T(8,128)(2,1)S(1)}, bf16[2,512,128]{2,1,0:T(8,128)(2,1)}, u32[]{:S(2)}) copy-start(bf16[2,512,128]{2,1,0:T(8,128)(2,1)} %get-tuple-element.427) | copy-start | bytes 786436 | tf_op jit(solution)/shard_map/while
  229.2 5.8 %copy-start.5 = (bf16[2,512,128]{2,1,0:T(8,128)(2,1)S(1)}, bf16[2,512,128]{2,1,0:T(8,128)(2,1)}, u32[]{:S(2)}) copy-start(bf16[2,512,128]{2,1,0:T(8,128)(2,1)} %get-tuple-element.427) | copy-start | bytes 786436 | tf_op jit(solution)/shard_map/while
  236.7 70.1 %copy-start.1 = (bf16[1024,1024]{1,0:T(8,128)(2,1)S(1)}, bf16[1024,1024]{1,0:T(8,128)(2,1)}, u32[]{:S(2)}) copy-start(bf16[1024,1024]{1,0:T(8,128)(2,1)} %param.16) | copy-start | bytes 6291460
Sparse Core Ops, SparseCore 0:
  166.1 55.5 all-gather.1
where the time goes:
time: 315 us
  matrix products  89.5 us (28%)
  waiting for transfers between devices  75.3 us (24%)
  blocking collectives  65.8 us (21%)
  local copies, waits for them, and re-layouts  32.6 us (10%)
  other arithmetic  25.9 us (8%)
  between operations  16 us (5%)
  starting transfers between devices  6.88 us (2%)
    psum x1, blocking collectives, body(): lax.psum(jnp.sum(local_score_terms), ('ens', 'space'))  65.8 us
    all_gather x1, waiting for transfers between devices, body(): member_group = lax.all_gather(predict_states, 'ens', axis=0, tiled=True)  55.7 us
    sub x2, matrix products, one_block(): expo = jnp.exp(scores - top)  37.9 us
    dot_general x2, matrix products, one_block(): jnp.einsum('hqk,khd->qhd', weights, value_piece, preferred_element_type=j...  30.1 us
    dynamic_slice x10, local copies, waits for them, and re-layouts, body(): lax.map(step_forward, (hidden_state, query_block, window_keys, window_val...  26.1 us
    ppermute x1, waiting for transfers between devices, padded(): before = lax.ppermute(last, axis, up)  15.2 us
    dot_general x3, matrix products, project(): jnp.einsum('mrd,de->mre', source, weight, preferred_element_type=jnp.floa...  10.9 us
    reduce_sum x2, other arithmetic, pairwise_member_terms(): jnp.sum(spread_of(differ)) / (2 * (member_states - 1))  8.38 us
  transfers between devices with their start and end apart: 3, of which 3 were waited for; matrix products, arithmetic and copies ran while one was open for 2% of the time, Pallas kernels for 0%

commit v1 on v0

v1 whole, which is shorter than its diff:
```python
import functools
import math

import jax
import jax.numpy as jnp
from jax import lax
from jax.experimental import pallas as pl
from jax.experimental.pallas import tpu as pltpu
from jax.sharding import PartitionSpec as P

HEADS = 16
WIN = 256
SMOOTH = 0.25
EPS = 1e-5
SUB = 128
UNROLL = 4
LOW, HIGH = 2.0**-80, 2.0**100
BF, F32 = jnp.bfloat16, jnp.float32
VMEM = pl.BlockSpec(memory_space=pltpu.VMEM)
NT = (((1,), (1,)), ((), ()))


def params():
    return pltpu.CompilerParams(vmem_limit_bytes=56 * 2**20)


def normed(rows, noise):
    hidden = rows.astype(F32) + noise
    return (hidden * lax.rsqrt(jnp.mean(hidden * hidden, axis=-1, keepdims=True) + EPS)).astype(BF)


def qkv_kernel(states, noise, w_query, w_key, w_value, query, keys, values, norm):
    members, rows, width = states.shape
    scale = math.log2(math.e) / math.sqrt(width // HEADS)

    @pl.when(pl.program_id(0) == 0)
    def _():
        for m in range(members):

            def piece(i, _):
                at = pl.ds(pl.multiple_of(i * SUB, SUB), SUB)
                norm[m, at] = normed(states[m, at], noise[m])
                return 0

            lax.fori_loop(0, rows // SUB, piece, 0)

    for m in range(members):
        x = norm[m]
        query[m] = (jnp.dot(x, w_query[...], preferred_element_type=F32) * scale).astype(BF)
        keys[m] = jnp.dot(x, w_key[...], preferred_element_type=F32).astype(BF)
        values[m] = jnp.dot(x, w_value[...], preferred_element_type=F32).astype(BF)


def qkv(states, noise, w_query, w_key, w_value):
    members, rows, width = states.shape
    cols = 256
    weight = pl.BlockSpec((width, cols), lambda j: (0, j))
    out = pl.BlockSpec((members, rows, cols), lambda j: (0, 0, j))
    return pl.pallas_call(
        qkv_kernel,
        grid=(width // cols,),
        out_shape=[jax.ShapeDtypeStruct(states.shape, BF)] * 3,
        in_specs=[
            pl.BlockSpec(states.shape, lambda j: (0, 0, 0)),
            pl.BlockSpec(noise.shape, lambda j: (0, 0, 0)),
            weight,
            weight,
            weight,
        ],
        out_specs=[out] * 3,
        scratch_shapes=[pltpu.VMEM(states.shape, BF)],
        compiler_params=params(),
        cost_estimate=pl.CostEstimate(
            flops=6 * members * rows * width * width, bytes_accessed=8 * 2**20, transcendentals=0
        ),
        name="own_qkv",
    )(states, noise, w_query, w_key, w_value)


def attend_kernel(
    place, states, noise, above, below, query, keys, values, w_key, w_value, w_out, w_decode,
    forecast, norm, halo_k, halo_v, kk, vv, mixed, bad,
):
    members, rows, width = states.shape
    pairs = width // SUB
    subs = rows // SUB
    pad = WIN // SUB
    span = 2 * pad + 1
    total = subs + 2 * pad
    lane = lax.broadcasted_iota(jnp.int32, (SUB, SUB), 1)
    row = lax.broadcasted_iota(jnp.int32, (SUB, SUB), 0)
    left = lane < SUB // 2
    zero = jnp.zeros((SUB, SUB), BF)
    one = jnp.ones((SUB, SUB), BF)
    starts = place[0] == 0
    ends = place[0] == place[1] - 1

    def absent(j):
        return starts if j < pad else ends

    def outside(j):
        return j < pad or j >= pad + subs

    for u in range(UNROLL):
        for j in range(total):
            unit = jnp.where(absent(j), zero, one) if outside(j) else one
            at = 2 * SUB * j
            vv[u, at : at + SUB, SUB:] = jnp.where(left, unit, zero)
            vv[u, at + SUB : at + 2 * SUB, SUB:] = jnp.where(left, zero, unit)

    def source(m, inner, halo, j, c):
        if j < pad:
            return halo[j * SUB : (j + 1) * SUB, c]
        if j < pad + subs:
            return inner[m, (j - pad) * SUB : (j - pad + 1) * SUB, c]
        return halo[(j - subs) * SUB : (j - subs + 1) * SUB, c]

    def pack(m, u, pair):
        c = pl.ds(pl.multiple_of(pair * SUB, SUB), SUB)
        for j in range(total):
            at = 2 * SUB * j
            key = source(m, keys, halo_k, j, c)
            value = source(m, values, halo_v, j, c)
            if outside(j):
                value = jnp.where(absent(j), zero, value)
            kk[u, at : at + SUB] = jnp.where(left, key, zero)
            kk[u, at + SUB : at + 2 * SUB] = jnp.where(left, zero, key)
            vv[u, at : at + SUB, :SUB] = jnp.where(left, value, zero)
            vv[u, at + SUB : at + 2 * SUB, :SUB] = jnp.where(left, zero, value)

    def masked(s, j):
        if j == 0:
            return jnp.where(lane >= row, s, -1e30)
        if j == span - 1:
            return jnp.where(lane <= row, s, -1e30)
        return s

    def block(m, u, pair, a):
        c = pl.ds(pl.multiple_of(pair * SUB, SUB), SUB)
        at = slice(2 * SUB * a, 2 * SUB * (a + span))
        s = lax.dot_general(
            query[m, a * SUB : (a + 1) * SUB, c], kk[u, at], NT, preferred_element_type=F32
        )
        parts = []
        for j in range(2 * span):
            parts.append(jnp.exp2(masked(s[:, j * SUB : (j + 1) * SUB], j // 2)).astype(BF))
        o = jnp.dot(jnp.concatenate(parts, axis=1), vv[u, at], preferred_element_type=F32)
        norms = o[:, SUB:]
        mixed[a * SUB : (a + 1) * SUB, c] = (o[:, :SUB] / norms).astype(BF)
        bad[...] = jnp.where((norms > LOW) & (norms < HIGH), bad[...], 1.0)

    def safe_block(m, pair, a):
        c = pl.ds(pl.multiple_of(pair * SUB, SUB), SUB)
        q = query[m, a * SUB : (a + 1) * SUB, c]
        outs = []
        for side in range(2):
            mine = left if side == 0 else ~left
            scores, vals = [], []
            for j in range(a, a + span):
                key = source(m, keys, halo_k, j, c)
                s = lax.dot_general(
                    jnp.where(mine, q, zero), key, NT, preferred_element_type=F32
                )
                s = masked(s, j - a)
                if outside(j):
                    s = jnp.where(absent(j), -1e30, s)
                scores.append(s)
                vals.append(source(m, values, halo_v, j, c))
            s = jnp.concatenate(scores, axis=1)
            p = jnp.exp2(s - jnp.max(s, axis=-1, keepdims=True))
            norms = jnp.sum(p, axis=-1, keepdims=True)
            outs.append(
                jnp.dot(
                    (p / norms).astype(BF),
                    jnp.concatenate(vals, axis=0),
                    preferred_element_type=F32,
                )
            )
        mixed[a * SUB : (a + 1) * SUB, c] = jnp.where(left, outs[0], outs[1]).astype(BF)

    def member(m, _):
        for i in range(pad):
            at = slice(i * SUB, (i + 1) * SUB)
            norm[at] = normed(above[m, at], noise[m])
            norm[WIN + i * SUB : WIN + (i + 1) * SUB] = normed(below[m, at], noise[m])

        def halo(i, _):
            c = pl.ds(pl.multiple_of(i * 256, 256), 256)
            halo_k[:, c] = jnp.dot(norm[...], w_key[:, c], preferred_element_type=F32).astype(BF)
            halo_v[:, c] = jnp.dot(norm[...], w_value[:, c], preferred_element_type=F32).astype(BF)
            return 0

        lax.fori_loop(0, width // 256, halo, 0)
        bad[...] = jnp.zeros_like(bad)

        def heads(i, _):
            for u in range(UNROLL):
                pack(m, u, i * UNROLL + u)
            for u in range(UNROLL):
                for a in range(subs):
                    block(m, u, i * UNROLL + u, a)
            return 0

        lax.fori_loop(0, pairs // UNROLL, heads, 0)

        @pl.when(jnp.max(bad[...]) > 0.0)
        def _():
            def again(pair, _):
                for a in range(subs):
                    safe_block(m, pair, a)
                return 0

            lax.fori_loop(0, pairs, again, 0)

        for i in range(rows // 256):
            at = slice(i * 256, (i + 1) * 256)
            hidden = states[m, at].astype(F32) + noise[m]
            updated = hidden + jnp.dot(mixed[at], w_out[...], preferred_element_type=F32)
            out = jnp.dot(updated.astype(BF), w_decode[...], preferred_element_type=F32)
            share = rows // forecast.shape[0]
            each = 256 // share
            forecast[i * each : (i + 1) * each, m] = out.astype(BF).reshape(each, share, -1)
        return 0

    lax.fori_loop(0, members, member, 0)


def attend(place, states, noise, above, below, query, keys, values, w_key, w_value, w_out, w_decode, shares):
    members, rows, width = states.shape
    held = 2 * WIN + rows
    return pl.pallas_call(
        attend_kernel,
        out_shape=jax.ShapeDtypeStruct((shares, members, rows // shares, w_decode.shape[1]), BF),
        in_specs=[pl.BlockSpec(memory_space=pltpu.SMEM)] + [VMEM] * 11,
        out_specs=VMEM,
        scratch_shapes=[
            pltpu.VMEM((2 * WIN, width), BF),
            pltpu.VMEM((2 * WIN, width), BF),
            pltpu.VMEM((2 * WIN, width), BF),
            pltpu.VMEM((UNROLL, 2 * held, SUB), BF),
            pltpu.VMEM((UNROLL, 2 * held, 2 * SUB), BF),
            pltpu.VMEM((rows, width), BF),
            pltpu.VMEM((SUB, SUB), F32),
        ],
        compiler_params=params(),
        cost_estimate=pl.CostEstimate(
            flops=24 * members * rows * width * width // 2,
            bytes_accessed=20 * 2**20,
            transcendentals=members * rows * HEADS * 640,
        ),
        name="window_attention",
    )(place, states, noise, above, below, query, keys, values, w_key, w_value, w_out, w_decode)


def crps_kernel(place, gathered, target, grad, partial):
    groups, local, share, lanes = gathered.shape
    members = groups * local
    first = place[2] * share

    def piece(i, total):
        at = pl.ds(pl.multiple_of(i * 16, 16), 16)
        out = []
        for half in range(2):
            cut = slice(half * 8, half * 8 + 8)
            goal = target[pl.ds(pl.multiple_of(first + i * 16 + half * 8, 8), 8)]
            pred = [gathered[m // local, m % local, at].astype(F32)[cut] for m in range(members)]
            slopes = [None] * members
            spread = jnp.zeros_like(goal)
            pull = []
            for a in range(members):
                delta = pred[a] - goal
                square = delta * delta + SMOOTH * SMOOTH
                inv = lax.rsqrt(square)
                pull.append(delta * inv)
                total = total + square * inv
                for b in range(a + 1, members):
                    delta = pred[a] - pred[b]
                    square = delta * delta + SMOOTH * SMOOTH
                    inv = lax.rsqrt(square)
                    f = delta * inv
                    spread = spread + square * inv
                    slopes[a] = f if slopes[a] is None else slopes[a] + f
                    slopes[b] = -f if slopes[b] is None else slopes[b] - f
            total = total - (2.0 * spread + members * SMOOTH) / (2 * (members - 1))
            out.append([pull[a] - slopes[a] / (members - 1) for a in range(members)])
        for m in range(members):
            grad[m // local, m % local, at] = jnp.concatenate([out[0][m], out[1][m]], 0).astype(BF)
        return total

    total = lax.fori_loop(0, share // 16, piece, jnp.zeros((8, lanes), F32))
    partial[...] = jnp.sum(total, axis=0, keepdims=True)


def crps(place, gathered, target):
    return pl.pallas_call(
        crps_kernel,
        out_shape=[
            jax.ShapeDtypeStruct(gathered.shape, BF),
            jax.ShapeDtypeStruct((1, gathered.shape[-1]), F32),
        ],
        in_specs=[pl.BlockSpec(memory_space=pltpu.SMEM), VMEM, VMEM],
        out_specs=[VMEM, VMEM],
        compiler_params=params(),
        name="fair_crps",
    )(place, gathered, target)


def back_kernel(slopes, w_decode, grad):
    shares, _, share, lanes = slopes.shape
    rows = slopes[:, 0].reshape(shares * share, lanes)
    grad[0] = lax.dot_general(rows, w_decode[...], NT, preferred_element_type=F32).astype(BF)


def back(slopes, w_decode):
    shares, members, share, lanes = slopes.shape
    width = w_decode.shape[0]
    cols = 512
    return pl.pallas_call(
        back_kernel,
        grid=(members, width // cols),
        out_shape=jax.ShapeDtypeStruct((members, shares * share, width), BF),
        in_specs=[
            pl.BlockSpec((shares, 1, share, lanes), lambda m, j: (0, m, 0, 0)),
            pl.BlockSpec((cols, lanes), lambda m, j: (j, 0)),
        ],
        out_specs=pl.BlockSpec((1, shares * share, cols), lambda m, j: (m, 0, j)),
        compiler_params=params(),
        cost_estimate=pl.CostEstimate(
            flops=2 * members * shares * share * width * lanes,
            bytes_accessed=3 * 2**20,
            transcendentals=0,
        ),
        name="state_grad",
    )(slopes, w_decode)


def body(states, member_noise, w_query, w_key, w_value, w_out, w_decode, target):
    members, rows, width = states.shape
    ens, space = lax.axis_size("ens"), lax.axis_size("space")
    place = jnp.stack([lax.axis_index("space"), jnp.int32(space), lax.axis_index("ens")])
    noise = member_noise[:, None, :]
    up = [(i, i + 1) for i in range(space - 1)]
    down = [(i + 1, i) for i in range(space - 1)]
    above = lax.ppermute(states[:, rows - WIN :], "space", up)
    below = lax.ppermute(states[:, :WIN], "space", down)
    query, keys, values = qkv(states, noise, w_query, w_key, w_value)
    forecast = attend(
        place, states, noise, above, below, query, keys, values, w_key, w_value, w_out, w_decode, ens
    )
    gathered = lax.all_to_all(forecast, "ens", 0, 0)
    slopes, partial = crps(place, gathered, target)
    mine = lax.all_to_all(slopes, "ens", 0, 0)
    parts = lax.all_to_all(
        jnp.broadcast_to(partial, (ens * space, 1, partial.shape[-1])), ("ens", "space"), 0, 0
    )
    loss = jnp.sum(parts) / (members * ens * rows * space * w_decode.shape[1])
    return back(mine, w_decode), loss


def solution(mesh):
    in_specs = (P("ens", "space", None), P("ens", None), P(), P(), P(), P(), P(), P("space", None))
    out_specs = (P("ens", "space", None), P())
    return jax.shard_map(body, mesh=mesh, in_specs=in_specs, out_specs=out_specs, check_vma=False)
```

time: 315 us -> 164 us (0.52)
  Pallas kernels: 0 us -> 107 us
  matrix products: 89.5 us -> 0 us
  waiting for transfers between devices: 75.3 us -> 5.96 us
  blocking collectives: 65.8 us -> 31.6 us
  local copies, waits for them, and re-layouts: 32.6 us -> 4.71 us
  other arithmetic: 25.9 us -> 1.22 us
  between operations: 16 us -> 2.48 us
  starting transfers between devices: 6.88 us -> 10.3 us
    pallas_call x0 -> x4, Pallas kernels: none -> 107 us  [the longest x1 87.5 us: attend(): pl.pallas_call(attend_kernel, out_shape=jax.ShapeDtypeStruct((shares, mem...]
    psum x1 -> x0, blocking collectives: 65.8 us -> none  [body(): lax.psum(jnp.sum(local_score_terms), ('ens', 'space'))]
    all_gather x1 -> x0, waiting for transfers between devices: 55.7 us -> none  [body(): member_group = lax.all_gather(predict_states, 'ens', axis=0, tiled=True)]
    dot_general x8 -> x0, matrix products: 51.5 us -> none  [the longest x2 30.1 us: one_block(): jnp.einsum('hqk,khd->qhd', weights, value_piece, preferred_element_type=j...]
    sub x2 -> x0, matrix products: 37.9 us -> none  [one_block(): expo = jnp.exp(scores - top)]
    all_to_all x0 -> x2, blocking collectives: none -> 31.6 us  [the longest x1 16.5 us: body(): lax.all_to_all(jnp.broadcast_to(partial, (ens * space, 1, partial.shape[-...]
    dynamic_slice x10 -> x0, local copies, waits for them, and re-layouts: 26.1 us -> none  [body(): lax.map(step_forward, (hidden_state, query_block, window_keys, window_val...]
    ppermute x2, waiting for transfers between devices: 19.6 us -> 0.01 us  [the longest x1 0.01 us: body(): below = lax.ppermute(states[:, :WIN], 'space', down)]
  transfers between devices with their start and end apart: 3 -> 3, of which waited for: 3 -> 1; matrix products, arithmetic and copies ran while one was open for 2% -> 1% of each run, Pallas kernels for 0% -> 7%
where the time goes in v1:
time: 164 us; the launch traced here: 163 us
  Pallas kernels  107 us (65%)
  blocking collectives  31.6 us (19%)
  starting transfers between devices  10.3 us (6%)
  waiting for transfers between devices  5.96 us (4%)
  local copies, waits for them, and re-layouts  4.71 us (3%)
  between operations  2.48 us (2%)
    pallas_call x1, Pallas kernels, attend(): pl.pallas_call(attend_kernel, out_shape=jax.ShapeDtypeStruct((shares, mem...  87.5 us
    all_to_all x1, blocking collectives, body(): lax.all_to_all(jnp.broadcast_to(partial, (ens * space, 1, partial.shape[-...  16.5 us
    all_to_all x1, blocking collectives, body(): gathered = lax.all_to_all(forecast, 'ens', 0, 0)  15.1 us
    pallas_call x1, Pallas kernels, qkv(): pl.pallas_call(qkv_kernel, grid=(width // cols,), out_shape=[jax.ShapeDty...  11.9 us
    all_to_all x1, waiting for transfers between devices, body(): mine = lax.all_to_all(slopes, 'ens', 0, 0)  5.96 us
    pallas_call x1, Pallas kernels, back(): pl.pallas_call(back_kernel, grid=(members, width // cols), out_shape=jax....  4.08 us
    ppermute x1, starting transfers between devices, body(): above = lax.ppermute(states[:, rows - WIN:], 'space', up)  3.53 us
    all_to_all x1, starting transfers between devices, body(): mine = lax.all_to_all(slopes, 'ens', 0, 0)  3.41 us
  transfers between devices with their start and end apart: 3, of which 1 were waited for; matrix products, arithmetic and copies ran while one was open for 1% of the time, Pallas kernels for 7%

profile of v1, /device:TPU:1, one launch (start us, length us, event | category | flops | bytes accessed | tf_op | source)
XLA Modules:
  0.0 162.9 jit_solution(757521548411012794)
XLA Ops:
  0.6 0.0 copy-start.1
  0.6 1.7 %fusion = (bf16[2,256,1024]{2,1,0:T(8,128)(2,1)S(1)}, bf16[2,256,1024]{2,1,0:T(8,128)(2,1)S(1)}) fusion(bf16[2,512,1024]{2,1,0:T(8,128)(2,1)} %states.3), kind=kLoop, calls=%fused_computation.1 | loop fusion | bytes 4194304 | tf_op jit(solution)/shard_map/slice | solution.py:345
  2.4 3.3 %collective-permute-start.1 = (bf16[2,256,1024]{2,1,0:T(8,128)(2,1)S(1)}, bf16[2,256,1024]{2,1,0:T(8,128)(2,1)S(1)}, u32[]{:S(2)}, u32[]{:S(2)}) collective-permute-start(bf16[2,256,1024]{2,1,0:T(8,128)(2,1)S(1)} %get-tuple-element.12), channel_id=1, source_target_pairs={{1,0},{2,1},{3,2},{4,3},{5,4},{6,5},{7,6},{8,7},{9,8},{10,9},{11,1... | collective-permute-start | bytes 3145736 | tf_op jit(solution)/shard_map/ppermute | solution.py:345
  5.7 3.5 %collective-permute-start = (bf16[2,256,1024]{2,1,0:T(8,128)(2,1)S(1)}, bf16[2,256,1024]{2,1,0:T(8,128)(2,1)}, u32[]{:S(2)}, u32[]{:S(2)}) collective-permute-start(bf16[2,256,1024]{2,1,0:T(8,128)(2,1)S(1)} %get-tuple-element.13), channel_id=1, source_target_pairs={{0,1},{1,2},{2,3},{3,4},{4,5},{5,6},{6,7},{7,8},{8,9},{9,10},{10,1... | collective-permute-start | bytes 3145736 | tf_op jit(solution)/shard_map/ppermute | solution.py:344
  9.2 0.0 copy-done.1
  9.2 0.6 broadcast_in_dim.6.noise
  9.8 0.6 pad_add_fusion.place
  10.5 11.9 %own_qkv.1 = (bf16[2,512,1024]{2,1,0:T(8,128)(2,1)}, bf16[2,512,1024]{2,1,0:T(8,128)(2,1)}, bf16[2,512,1024]{2,1,0:T(8,128)(2,1)}) custom-call(bf16[2,512,1024]{2,1,0:T(8,128)(2,1)} %states.3, f32[2,1,1024]{2,1,0:T(1,128)} %broadcast_in_dim.6.noise, bf16[1024,1024]{1,0:T(8,128)(2,1)} %w_query.1, bf16[1024,1024]{1,0:T(8,128)(2,1)} %w_key.3, ...), custom_call_target="tpu_custom_call" | custom-call | flops 6442450944 | bytes 8388608 | tf_op jit(solution)/shard_map/own_qkv/pallas_call | solution.py:59
  22.3 0.0 collective-permute-done.1.below
  22.3 0.0 copy-start.2
  22.3 0.0 collective-permute-done.above
  22.3 1.0 copy-done.2
  23.3 87.5 %window_attention.1 = bf16[8,2,64,128]{3,2,1,0:T(8,128)(2,1)} custom-call(s32[3]{0:T(128)} %pad_add_fusion.place, bf16[2,512,1024]{2,1,0:T(8,128)(2,1)} %states.3, f32[2,1,1024]{2,1,0:T(1,128)} %broadcast_in_dim.6.noise, bf16[2,256,1024]{2,1,0:T(8,128)(2,1)} %collective-permute-done.above, bf16[2,256,1024]{2,1,0:T(8,128)(2,1)} %copy-done.2, ...), custom_call_target="tpu_custom_call" | custom-call | flops 12884901888 | bytes 20971520 | tf_op jit(solution)/shard_map/window_attention/pallas_call | solution.py:231
  110.8 15.1 %all_to_all.15.gathered = bf16[8,2,64,128]{3,2,1,0:T(8,128)(2,1)} all-to-all(bf16[8,2,64,128]{3,2,1,0:T(8,128)(2,1)} %window_attention.1), channel_id=1, replica_groups=mesh['ens'=8,'space'=16] {'ens'}, dimensions={0} | all-to-all | bytes 524288 | tf_op jit(solution)/shard_map/all_to_all | solution.py:350
  125.9 3.2 %fair_crps.1 = (bf16[8,2,64,128]{3,2,1,0:T(8,128)(2,1)}, f32[1,128]{1,0:T(1,128)}) custom-call(s32[3]{0:T(128)} %pad_add_fusion.place, bf16[8,2,64,128]{3,2,1,0:T(8,128)(2,1)} %all_to_all.15.gathered, f32[512,128]{1,0:T(8,128)} %target.1), custom_call_target="tpu_custom_call" | custom-call | tf_op jit(solution)/shard_map/fair_crps/pallas_call | solution.py:295
  129.1 0.7 broadcast_in_dim.7
  129.8 16.5 %all_to_all.16 = f32[128,1,128]{2,1,0:T(1,128)S(1)} all-to-all(f32[128,1,128]{2,1,0:T(1,128)S(1)} %broadcast_in_dim.7), channel_id=1, replica_groups=mesh['ens'=8,'space'=16] {'ens','space'}, dimensions={0} | all-to-all | bytes 131072 | tf_op jit(solution)/shard_map/all_to_all | solution.py:353
  146.4 3.4 %all-to-all-start.1 = ((bf16[8,2,64,128]{3,2,1,0:T(8,128)(2,1)}), bf16[8,2,64,128]{3,2,1,0:T(8,128)(2,1)S(1)}, u32[]{:S(2)}, u32[]{:S(2)}) async-start(bf16[8,2,64,128]{3,2,1,0:T(8,128)(2,1)} %get-tuple-element.10), calls=%async_computation.1 | async-start | bytes 524288 | tf_op jit(solution)/shard_map/all_to_all | solution.py:352
  149.8 0.6 reduce_sum.9
  151.0 6.0 %all-to-all-done.1.slopes = bf16[8,2,64,128]{3,2,1,0:T(8,128)(2,1)S(1)} async-done(((bf16[8,2,64,128]{3,2,1,0:T(8,128)(2,1)}), bf16[8,2,64,128]{3,2,1,0:T(8,128)(2,1)S(1)}, u32[]{:S(2)}, u32[]{:S(2)}) %all-to-all-start.1) | async-done | bytes 262176 | tf_op jit(solution)/shard_map/all_to_all | solution.py:352
  157.0 0.0 copy-start
  157.0 0.7 copy-done
  157.7 4.1 %state_grad.1 = bf16[2,512,1024]{2,1,0:T(8,128)(2,1)} custom-call(bf16[8,2,64,128]{3,2,1,0:T(8,128)(2,1)} %copy-done, bf16[1024,128]{1,0:T(8,128)(2,1)} %w_decode.3), custom_call_target="tpu_custom_call" | custom-call | flops 268435456 | bytes 3145728 | tf_op jit(solution)/shard_map/state_grad/pallas_call | solution.py:318
Async XLA Ops:
  0.6 8.6 %copy-start.1 = (f32[2,1024]{1,0:T(2,128)S(1)}, f32[2,1024]{1,0:T(2,128)}, u32[]{:S(2)}) copy-start(f32[2,1024]{1,0:T(2,128)} %param.9) | copy-start | bytes 24580
  2.4 19.9 %collective-permute-start.1 = (bf16[2,256,1024]{2,1,0:T(8,128)(2,1)S(1)}, bf16[2,256,1024]{2,1,0:T(8,128)(2,1)S(1)}, u32[]{:S(2)}, u32[]{:S(2)}) collective-permute-start(bf16[2,256,1024]{2,1,0:T(8,128)(2,1)S(1)} %get-tuple-element.12), channel_id=1, source_target_pairs={{1,0},{2,1},{3,2},{4,3},{5,4},{6,5},{7,6},{8,7},{9,8},{10,9},{11,1... | collective-permute-start | bytes 3145736 | tf_op jit(solution)/shard_map/ppermute | solution.py:345
  5.7 16.6 %collective-permute-start = (bf16[2,256,1024]{2,1,0:T(8,128)(2,1)S(1)}, bf16[2,256,1024]{2,1,0:T(8,128)(2,1)}, u32[]{:S(2)}, u32[]{:S(2)}) collective-permute-start(bf16[2,256,1024]{2,1,0:T(8,128)(2,1)S(1)} %get-tuple-element.13), channel_id=1, source_target_pairs={{0,1},{1,2},{2,3},{3,4},{4,5},{5,6},{6,7},{7,8},{8,9},{9,10},{10,1... | collective-permute-start | bytes 3145736 | tf_op jit(solution)/shard_map/ppermute | solution.py:344
  22.3 1.0 copy-start.2
  146.4 10.6 %all-to-all-start.1 = ((bf16[8,2,64,128]{3,2,1,0:T(8,128)(2,1)}), bf16[8,2,64,128]{3,2,1,0:T(8,128)(2,1)S(1)}, u32[]{:S(2)}, u32[]{:S(2)}) async-start(bf16[8,2,64,128]{3,2,1,0:T(8,128)(2,1)} %get-tuple-element.10), calls=%async_computation.1 | async-start | bytes 524288 | tf_op jit(solution)/shard_map/all_to_all | solution.py:352
  157.0 0.7 copy-start

commit v2 on v1

v2 whole, which is shorter than its diff:
```python
import functools
import math

import jax
import jax.numpy as jnp
from jax import lax
from jax.experimental import pallas as pl
from jax.experimental.pallas import tpu as pltpu
from jax.sharding import PartitionSpec as P

HEADS = 16
WIN = 256
SMOOTH = 0.25
EPS = 1e-5
LOG2E = math.log2(math.e)
SUB = 128
UNROLL = 4
TAIL = 16
LOW, HIGH = 2.0**-80, 2.0**100
BF, F32 = jnp.bfloat16, jnp.float32
VMEM = pl.BlockSpec(memory_space=pltpu.VMEM)
HBM = pl.BlockSpec(memory_space=pltpu.HBM)
NT = (((1,), (1,)), ((), ()))


def params(mib):
    return pltpu.CompilerParams(vmem_limit_bytes=mib * 2**20)


def normed(rows, noise):
    hidden = rows.astype(F32) + noise
    return (hidden * lax.rsqrt(jnp.mean(hidden * hidden, axis=-1, keepdims=True) + EPS)).astype(BF)


def split(x, terms):
    parts = []
    for _ in range(terms):
        parts.append(x.astype(BF))
        x = x - parts[-1].astype(F32)
    return parts


def edges_kernel(states, far, near, sems):
    rows = states.shape[1]
    even = lax.axis_index("space") % 2 == 0
    first, last = pl.ds(0, WIN), pl.ds(rows - WIN, WIN)

    def move(out, back):
        copies = [
            pltpu.make_async_copy(states.at[0, out], far, sems.at[0]),
            pltpu.make_async_copy(states.at[:, back], near, sems.at[1]),
        ]
        for copy in copies:
            copy.start()
        for copy in copies:
            copy.wait()

    @pl.when(even)
    def _():
        move(first, last)

    @pl.when(~even)
    def _():
        move(last, first)


def edges(states):
    members, _, width = states.shape
    return pl.pallas_call(
        edges_kernel,
        out_shape=[
            jax.ShapeDtypeStruct((WIN, width), BF),
            jax.ShapeDtypeStruct((members, WIN, width), BF),
        ],
        in_specs=[HBM],
        out_specs=[VMEM] * 2,
        scratch_shapes=[pltpu.SemaphoreType.DMA((2,))],
        compiler_params=params(4),
        name="edges",
    )(pltpu.with_memory_space_constraint(states, pltpu.HBM))


def qkv_kernel(
    states, noise, w_query, w_key, w_value, query, keys, values, far, held_key, held_value,
    norm, shift, held_query, sems,
):
    members, rows, width = states.shape
    even = lax.axis_index("space") % 2 == 0
    scale = 1.0 / math.sqrt(width // HEADS)
    step = 256
    pieces = [(m, pl.ds(i * step, step)) for m in range(members) for i in range(rows // step)]
    moves = [(noise, shift), (w_query, held_query), (w_key, held_key), (w_value, held_value)]
    copies = [pltpu.make_async_copy(a, b, sems.at[i]) for i, (a, b) in enumerate(moves)]
    copies[0].start()
    copies[1].start()
    copies[0].wait()
    for m, at in pieces[:1]:
        norm[m, at] = normed(states[m, at], shift[m : m + 1])
    copies[1].wait()
    copies[2].start()
    copies[3].start()
    for i, (m, at) in enumerate(pieces):
        x = norm[m, at]
        query[m, at] = (jnp.dot(x, held_query[...], preferred_element_type=F32) * scale).astype(BF)
        for later, part in pieces[i + 1 : i + 2]:
            norm[later, part] = normed(states[later, part], shift[later : later + 1])
    for m in range(1, members):
        far[m - 1] = jnp.where(even, states[m, :WIN], states[m, rows - WIN :])
    copies[2].wait()
    for m, at in pieces:
        keys[m, at] = jnp.dot(norm[m, at], held_key[...], preferred_element_type=F32).astype(BF)
    copies[3].wait()
    for m, at in pieces:
        values[m, at] = jnp.dot(norm[m, at], held_value[...], preferred_element_type=F32).astype(BF)


def qkv(states, noise, w_query, w_key, w_value):
    members, rows, width = states.shape
    return pl.pallas_call(
        qkv_kernel,
        out_shape=[jax.ShapeDtypeStruct(states.shape, BF)] * 3
        + [jax.ShapeDtypeStruct((members - 1, WIN, width), BF)]
        + [pltpu.VMEM(x.shape, BF) for x in (w_key, w_value)],
        in_specs=[VMEM] + [HBM] * 4,
        out_specs=[VMEM] * 6,
        scratch_shapes=[
            pltpu.VMEM(states.shape, BF),
            pltpu.VMEM(noise.shape, F32),
            pltpu.VMEM(w_query.shape, BF),
            pltpu.SemaphoreType.DMA((4,)),
        ],
        compiler_params=params(20),
        cost_estimate=pl.CostEstimate(
            flops=6 * members * rows * width * width, bytes_accessed=8 * 2**20, transcendentals=0
        ),
        name="own_qkv",
    )(states, *[pltpu.with_memory_space_constraint(x, pltpu.HBM) for x in (noise, w_query, w_key, w_value)])


def attend_kernel(
    m, states, noise, inner, outer, query, keys, values, w_key, w_value, w_out, w_decode, earlier,
    forecast, w_both, halo_k, halo_v, kk, vv, mixed, bad,
):
    members, rows, width = states.shape
    pairs = width // SUB
    subs = rows // SUB
    pad = WIN // SUB
    span = 2 * pad + 1
    total = subs + 2 * pad
    lane = lax.broadcasted_iota(jnp.int32, (SUB, SUB), 1)
    row = lax.broadcasted_iota(jnp.int32, (SUB, SUB), 0)
    left = lane < SUB // 2
    zero = jnp.zeros((SUB, SUB), BF)
    one = jnp.ones((SUB, SUB), BF)
    place = lax.axis_index("space")
    even = place % 2 == 0
    starts = place == 0
    ends = place == lax.axis_size("space") - 1

    def absent(j):
        return starts if j < pad else ends

    def outside(j):
        return j < pad or j >= pad + subs

    for u in range(UNROLL):
        for j in range(total):
            unit = jnp.where(absent(j), zero, one) if outside(j) else one
            at = 2 * SUB * j
            vv[u, at : at + SUB, SUB:] = jnp.where(left, unit, zero)
            vv[u, at + SUB : at + 2 * SUB, SUB:] = jnp.where(left, zero, unit)

    def source(m, inner, halo, j, c):
        if j < pad:
            return halo[j * SUB : (j + 1) * SUB, c]
        if j < pad + subs:
            return inner[m, (j - pad) * SUB : (j - pad + 1) * SUB, c]
        return halo[(j - subs) * SUB : (j - subs + 1) * SUB, c]

    def pack(m, u, pair):
        c = pl.ds(pl.multiple_of(pair * SUB, SUB), SUB)
        for j in range(total):
            at = 2 * SUB * j
            key = source(m, keys, halo_k, j, c)
            value = source(m, values, halo_v, j, c)
            if outside(j):
                value = jnp.where(absent(j), zero, value)
            kk[u, at : at + SUB] = jnp.where(left, key, zero)
            kk[u, at + SUB : at + 2 * SUB] = jnp.where(left, zero, key)
            vv[u, at : at + SUB, :SUB] = jnp.where(left, value, zero)
            vv[u, at + SUB : at + 2 * SUB, :SUB] = jnp.where(left, zero, value)

    def masked(s, j):
        if j == 0:
            return jnp.where(lane >= row, s, -1e30)
        if j == span - 1:
            return jnp.where(lane <= row, s, -1e30)
        return s

    def block(m, u, pair, a):
        c = pl.ds(pl.multiple_of(pair * SUB, SUB), SUB)
        at = slice(2 * SUB * a, 2 * SUB * (a + span))
        s = lax.dot_general(
            query[m, a * SUB : (a + 1) * SUB, c], kk[u, at], NT, preferred_element_type=F32
        )
        parts = []
        for j in range(2 * span):
            parts.append(jnp.exp2(masked(s[:, j * SUB : (j + 1) * SUB] * LOG2E, j // 2)).astype(BF))
        o = jnp.dot(jnp.concatenate(parts, axis=1), vv[u, at], preferred_element_type=F32)
        norms = o[:, SUB:]
        mixed[a * SUB : (a + 1) * SUB, c] = (o[:, :SUB] / norms).astype(BF)
        bad[...] = jnp.where((norms > LOW) & (norms < HIGH), bad[...], 1.0)

    def safe_block(m, pair, a):
        c = pl.ds(pl.multiple_of(pair * SUB, SUB), SUB)
        q = query[m, a * SUB : (a + 1) * SUB, c]
        outs = []
        for side in range(2):
            mine = left if side == 0 else ~left
            scores, vals = [], []
            for j in range(a, a + span):
                key = source(m, keys, halo_k, j, c)
                own = jnp.where(mine, q, zero)
                s = lax.dot_general(own, key, NT, preferred_element_type=F32)
                s = masked(s * LOG2E, j - a)
                if outside(j):
                    s = jnp.where(absent(j), -1e30, s)
                scores.append(s)
                vals.append(source(m, values, halo_v, j, c))
            s = jnp.concatenate(scores, axis=1)
            p = jnp.exp2(s - jnp.max(s, axis=-1, keepdims=True))
            norms = jnp.sum(p, axis=-1, keepdims=True)
            outs.append(
                jnp.dot(
                    (p / norms).astype(BF),
                    jnp.concatenate(vals, axis=0),
                    preferred_element_type=F32,
                )
            )
        mixed[a * SUB : (a + 1) * SUB, c] = jnp.where(left, outs[0], outs[1]).astype(BF)

    shift = noise[m : m + 1]
    for side in range(2):
        x = normed(jnp.where(even == (side == 0), outer[...], inner[m]), shift)
        at = slice(side * WIN, (side + 1) * WIN)
        halo_k[at] = jnp.dot(x, w_key[...], preferred_element_type=F32).astype(BF)
        halo_v[at] = jnp.dot(x, w_value[...], preferred_element_type=F32).astype(BF)
    bad[...] = jnp.zeros_like(bad)

    lanes = w_decode.shape[1]
    if m == 0:
        product = jnp.dot(w_out[...], w_decode[...], preferred_element_type=F32)
        w_both[:, :lanes], w_both[:, lanes:] = split(product, 2)
    else:
        w_both[...] = earlier[0][...]
        for i in range(m):
            forecast[:, i] = earlier[1][:, i]

    def heads(i, _):
        for u in range(UNROLL):
            pack(m, u, i * UNROLL + u)
        for u in range(UNROLL):
            for a in range(subs):
                block(m, u, i * UNROLL + u, a)
        return 0

    lax.fori_loop(0, pairs // UNROLL, heads, 0)

    @pl.when(jnp.max(bad[...]) > 0.0)
    def _():
        def again(pair, _):
            for a in range(subs):
                safe_block(m, pair, a)
            return 0

        lax.fori_loop(0, pairs, again, 0)

    constant = jnp.dot(
        jnp.concatenate([jnp.broadcast_to(x, (8, width)) for x in split(shift, 3)], axis=0),
        w_decode[...],
        preferred_element_type=F32,
    )
    constant = constant[0:1] + constant[8:9] + constant[16:17]
    for i in range(rows // 256):
        at = slice(i * 256, (i + 1) * 256)
        out = jnp.dot(mixed[at], w_both[...], preferred_element_type=F32)
        out = out[:, :lanes] + out[:, lanes:] + constant
        out = out + jnp.dot(states[m, at], w_decode[...], preferred_element_type=F32)
        share = rows // forecast.shape[0]
        each = 256 // share
        forecast[i * each : (i + 1) * each, m] = out.astype(BF).reshape(each, share, -1)


def attend(m, states, noise, inner, outer, query, keys, values, w_key, w_value, w_out, w_decode, shares, earlier):
    members, rows, width = states.shape
    held = 2 * WIN + rows
    lanes = w_decode.shape[1]
    taken = [] if earlier is None else list(earlier)

    def kernel(*refs):
        ins, rest = refs[:11], refs[11:]
        attend_kernel(m, *ins, rest[: len(taken)], *rest[len(taken) :])

    return pl.pallas_call(
        kernel,
        out_shape=[
            jax.ShapeDtypeStruct((shares, members, rows // shares, lanes), BF),
            jax.ShapeDtypeStruct((width, 2 * lanes), BF),
        ],
        in_specs=[VMEM] * (11 + len(taken)),
        out_specs=[VMEM] * 2,
        scratch_shapes=[
            pltpu.VMEM((2 * WIN, width), BF),
            pltpu.VMEM((2 * WIN, width), BF),
            pltpu.VMEM((UNROLL, 2 * held, SUB), BF),
            pltpu.VMEM((UNROLL, 2 * held, 2 * SUB), BF),
            pltpu.VMEM((rows, width), BF),
            pltpu.VMEM((SUB, SUB), F32),
        ],
        compiler_params=params(24),
        cost_estimate=pl.CostEstimate(
            flops=12 * rows * width * width,
            bytes_accessed=8 * 2**20,
            transcendentals=rows * HEADS * 640,
        ),
        name="window_attention",
    )(states, noise, inner, outer, query, keys, values, w_key, w_value, w_out, w_decode, *taken)


def crps_kernel(gathered, target, grad):
    groups, local, share, lanes = gathered.shape
    members = groups * local
    first = lax.axis_index("ens") * share

    def piece(i, total):
        at = pl.ds(pl.multiple_of(i * 16, 16), 16)
        out = []
        for half in range(2):
            cut = slice(half * 8, half * 8 + 8)
            goal = target[pl.ds(pl.multiple_of(first + i * 16 + half * 8, 8), 8)]
            pred = [gathered[m // local, m % local, at].astype(F32)[cut] for m in range(members)]
            slopes = [None] * members
            spread = jnp.zeros_like(goal)
            pull = []
            for a in range(members):
                delta = pred[a] - goal
                square = delta * delta + SMOOTH * SMOOTH
                inv = lax.rsqrt(square)
                pull.append(delta * inv)
                total = total + square * inv
                for b in range(a + 1, members):
                    delta = pred[a] - pred[b]
                    square = delta * delta + SMOOTH * SMOOTH
                    inv = lax.rsqrt(square)
                    f = delta * inv
                    spread = spread + square * inv
                    slopes[a] = f if slopes[a] is None else slopes[a] + f
                    slopes[b] = -f if slopes[b] is None else slopes[b] - f
            total = total - (2.0 * spread + members * SMOOTH) / (2 * (members - 1))
            out.append([pull[a] - slopes[a] / (members - 1) for a in range(members)])
        for m in range(members):
            to = pl.ds(pl.multiple_of(m % local * share + i * 16, 16), 16)
            grad[m // local, to] = jnp.concatenate([out[0][m], out[1][m]], 0).astype(BF)
        return total

    total = lax.fori_loop(0, share // 16, piece, jnp.zeros((8, lanes), F32))
    terms = split(jnp.sum(total, axis=0, keepdims=True), 3)
    row = lax.broadcasted_iota(jnp.int32, (TAIL, lanes), 0)
    tail = jnp.zeros((TAIL, lanes), F32)
    for i, term in enumerate(terms):
        tail = jnp.where(row == i, term.astype(F32), tail)
    for i in range(groups):
        grad[i, local * share :] = tail.astype(BF)


def crps(gathered, target):
    groups, local, share, lanes = gathered.shape
    return pl.pallas_call(
        crps_kernel,
        out_shape=jax.ShapeDtypeStruct((groups, local * share + TAIL, lanes), BF),
        in_specs=[VMEM, VMEM],
        out_specs=VMEM,
        compiler_params=params(8),
        name="fair_crps",
    )(gathered, target)


def back_kernel(members, slopes, w_decode, grad):
    shares, held, lanes = slopes.shape
    share = (held - TAIL) // members
    steps = pl.num_programs(0) // members
    each = shares // steps
    step = pl.program_id(0)
    at = pl.ds(pl.multiple_of(step // steps * share, 16), share)
    rows = slopes[pl.ds(step % steps * each, each), at].reshape(each * share, lanes)
    grad[0] = lax.dot_general(rows, w_decode[...], NT, preferred_element_type=F32).astype(BF)


def back(slopes, w_decode, members):
    shares, held, lanes = slopes.shape
    share = (held - TAIL) // members
    width = w_decode.shape[0]
    steps = 2
    rows = shares * share
    return pl.pallas_call(
        functools.partial(back_kernel, members),
        grid=(members * steps,),
        out_shape=jax.ShapeDtypeStruct((members, rows, width), BF),
        in_specs=[
            pl.BlockSpec(slopes.shape, lambda i: (0, 0, 0)),
            pl.BlockSpec(w_decode.shape, lambda i: (0, 0)),
        ],
        out_specs=pl.BlockSpec((1, rows // steps, width), lambda i: (i // steps, i % steps, 0)),
        compiler_params=params(12),
        cost_estimate=pl.CostEstimate(
            flops=2 * members * rows * width * lanes, bytes_accessed=3 * 2**20, transcendentals=0
        ),
        name="state_grad",
    )(slopes, w_decode)


def body(states, member_noise, w_query, w_key, w_value, w_out, w_decode, target):
    members, rows, width = states.shape
    ens, space = lax.axis_size("ens"), lax.axis_size("space")
    cross = [(i, i + 1) for i in range(1, space - 1, 2)]
    chip = [(i, i + 1) for i in range(0, space, 2)]
    both = lambda pairs: pairs + [(j, i) for i, j in pairs]
    far, near = edges(states)
    outer = [lax.ppermute(far, "space", both(cross))]
    inner = lax.ppermute(near, "space", both(chip))
    query, keys, values, far, w_key, w_value = qkv(
        states, member_noise, w_query, w_key, w_value
    )
    outer += [lax.ppermute(far[m], "space", both(cross)) for m in range(members - 1)]
    done = None
    for m in range(members):
        done = attend(
            m, states, member_noise, inner, outer[m], query, keys, values,
            w_key, w_value, w_out, w_decode, ens, done and (done[1], done[0]),
        )
    gathered = lax.all_to_all(done[0], "ens", 0, 0)
    slopes = lax.all_to_all(crps(gathered, target), "ens", 0, 0)
    held = slopes.shape[1] - TAIL
    part = jnp.sum(slopes[:, held : held + 3].astype(F32), axis=(0, 1))
    parts = lax.all_to_all(jnp.broadcast_to(part, (space, 1, part.shape[0])), "space", 0, 0)
    loss = jnp.sum(parts) / (members * ens * rows * space * w_decode.shape[1])
    return back(slopes, w_decode, members), loss


def solution(mesh):
    in_specs = (P("ens", "space", None), P("ens", None), P(), P(), P(), P(), P(), P("space", None))
    out_specs = (P("ens", "space", None), P())
    return jax.shard_map(body, mesh=mesh, in_specs=in_specs, out_specs=out_specs, check_vma=False)
```

time: 164 us -> 143 us (0.87)
  Pallas kernels: 107 us -> 94.6 us
  blocking collectives: 31.6 us -> 24.4 us
  starting transfers between devices: 10.3 us -> 17.2 us
  local copies, waits for them, and re-layouts: 4.71 us -> 0.62 us
  waiting for transfers between devices: 5.96 us -> 2.94 us
    pallas_call x4 -> x6, Pallas kernels: 107 us -> 94.6 us  [the longest x2 80.2 us: attend(): pl.pallas_call(kernel, out_shape=[jax.ShapeDtypeStruct((shares, members,...]
    all_to_all x2, blocking collectives: 31.6 us -> 24.4 us  [the longest x1 13.8 us: body(): gathered = lax.all_to_all(done[0], 'ens', 0, 0)]
    all_to_all x1, starting transfers between devices: 3.41 us -> 9.84 us  [body(): lax.all_to_all(jnp.broadcast_to(part, (space, 1, part.shape[0])), 'space'...]
    all_to_all x1, waiting for transfers between devices: 5.96 us -> 2.94 us  [body(): lax.all_to_all(jnp.broadcast_to(part, (space, 1, part.shape[0])), 'space'...]
    slice x1 -> x0, local copies, waits for them, and re-layouts: 1.72 us -> none  [body(): below = lax.ppermute(states[:, :WIN], 'space', down)]
    unnamed x6 -> x10, local copies, waits for them, and re-layouts: 1.7 us -> 0.02 us
    ppermute x2 -> x3, starting transfers between devices: 6.86 us -> 7.36 us  [the longest x1 3.69 us: body(): outer = [lax.ppermute(far, 'space', both(cross))]]
  transfers between devices with their start and end apart: 3 -> 4, of which waited for: 1 -> 1; matrix products, arithmetic and copies ran while one was open for 1% -> 0% of each run, Pallas kernels for 7% -> 36%
where the time goes in v2:
time: 143 us
  Pallas kernels  94.6 us (66%)
  blocking collectives  24.4 us (17%)
  starting transfers between devices  17.2 us (12%)
  waiting for transfers between devices  2.94 us (2%)
  between operations  2.52 us (2%)
    pallas_call x2, Pallas kernels, attend(): pl.pallas_call(kernel, out_shape=[jax.ShapeDtypeStruct((shares, members,...  80.2 us
    all_to_all x1, blocking collectives, body(): gathered = lax.all_to_all(done[0], 'ens', 0, 0)  13.8 us
    all_to_all x1, blocking collectives, body(): slopes = lax.all_to_all(crps(gathered, target), 'ens', 0, 0)  10.6 us
    all_to_all x1, starting transfers between devices, body(): lax.all_to_all(jnp.broadcast_to(part, (space, 1, part.shape[0])), 'space'...  9.84 us
    pallas_call x1, Pallas kernels, qkv(): pl.pallas_call(qkv_kernel, out_shape=[jax.ShapeDtypeStruct(states.shape,...  8.84 us
    ppermute x1, starting transfers between devices, body(): outer = [lax.ppermute(far, 'space', both(cross))]  3.69 us
    all_to_all x1, waiting for transfers between devices, body(): lax.all_to_all(jnp.broadcast_to(part, (space, 1, part.shape[0])), 'space'...  2.94 us
  transfers between devices with their start and end apart: 4, of which 1 were waited for; matrix products, arithmetic and copies ran while one was open for 0% of the time, Pallas kernels for 36%

profile of v2, /device:TPU:1, one launch (start us, length us, event | category | flops | bytes accessed | tf_op | source)
XLA Modules:
  0.0 142.9 jit_solution(3796547558146075495)
XLA Ops:
  0.6 0.0 copy-start
  0.6 1.6 %edges.1 = (bf16[256,1024]{1,0:T(8,128)(2,1)S(1)}, bf16[2,256,1024]{2,1,0:T(8,128)(2,1)S(1)}) custom-call(bf16[2,512,1024]{2,1,0:T(8,128)(2,1)} %refs_0_.3), custom_call_target="tpu_custom_call" | custom-call | tf_op jit(solution)/shard_map/edges/pallas_call | solution.py:69
  2.2 1.5 %collective-permute-start = (bf16[2,256,1024]{2,1,0:T(8,128)(2,1)S(1)}, bf16[2,256,1024]{2,1,0:T(8,128)(2,1)S(1)}, u32[]{:S(2)}, u32[]{:S(2)}) collective-permute-start(bf16[2,256,1024]{2,1,0:T(8,128)(2,1)S(1)} %get-tuple-element.13), channel_id=1, source_target_pairs={{0,1},{2,3},{4,5},{6,7},{8,9},{10,11},{12,13},{14,15},{1,0},{3,2},... | collective-permute-start | bytes 3145736 | tf_op jit(solution)/shard_map/ppermute | solution.py:430
  3.7 0.0 copy-start.2
  3.7 0.0 copy-start.3
  3.7 0.0 copy-start.4
  3.7 3.7 %collective-permute-start.2 = (bf16[256,1024]{1,0:T(8,128)(2,1)S(1)}, bf16[256,1024]{1,0:T(8,128)(2,1)S(1)}, u32[]{:S(2)}, u32[]{:S(2)}) collective-permute-start(bf16[256,1024]{1,0:T(8,128)(2,1)S(1)} %get-tuple-element.20), channel_id=1, source_target_pairs={{1,2},{3,4},{5,6},{7,8},{9,10},{11,12},{13,14},{2,1},{4,3},{6,5},{... | collective-permute-start | bytes 1572872 | tf_op jit(solution)/shard_map/ppermute | solution.py:429
  7.4 0.0 copy-done
  7.4 8.8 %own_qkv.1 = (bf16[2,512,1024]{2,1,0:T(8,128)(2,1)S(1)}, bf16[2,512,1024]{2,1,0:T(8,128)(2,1)S(1)}, bf16[2,512,1024]{2,1,0:T(8,128)(2,1)S(1)}, bf16[1,256,1024]{...) custom-call(bf16[2,512,1024]{2,1,0:T(8,128)(2,1)S(1)} %copy-done, ...), custom_call_target="tpu_custom_call" | custom-call | flops 6442450944 | bytes 8388608 | tf_op jit(solution)/shard_map/own_qkv/pallas_call | solution.py:119
  16.3 2.2 %collective-permute-start.1 = (bf16[256,1024]{1,0:T(8,128)(2,1)S(1)}, bf16[256,1024]{1,0:T(8,128)(2,1)S(1)}, u32[]{:S(2)}, u32[]{:S(2)}) collective-permute-start(bf16[256,1024]{1,0:T(8,128)(2,1)S(1)} %bitcast.2), channel_id=1, source_target_pairs={{1,2},{3,4},{5,6},{7,8},{9,10},{11,12},{13,14},{2,1},{4,3},{6,5},{... | collective-permute-start | bytes 1572872 | tf_op jit(solution)/shard_map/ppermute | solution.py:434
  18.4 0.0 collective-permute-done.2.refs_3_
  18.4 0.0 collective-permute-done.refs_2_
  18.5 0.0 copy-done.2
  18.5 0.0 copy-done.3
  18.5 0.0 copy-done.4
  18.5 40.2 %window_attention.2 = (bf16[8,2,64,128]{3,2,1,0:T(8,128)(2,1)S(1)}, bf16[1024,256]{1,0:T(8,128)(2,1)S(1)}) custom-call(bf16[2,512,1024]{2,1,0:T(8,128)(2,1)S(1)} %copy-done, f32[2,1024]{1,0:T(2,128)S(1)} %copy-done.4, bf16[2,256,1024]{2,1,0:T(8,128)(2,1)S(1)} %collective-permute-done.refs_2_, bf16[256,1024]{1,0:T(8,128)(2,1)S(1)} %collective-permute-done.2.refs_3_, ...), custom_call_target="tpu_custom_call" | custom-call | flops 6442450944 | bytes 8388608 | tf_op jit(solution)/shard_map/window_attention/pallas_call | solution.py:304
  58.6 0.0 collective-permute-done.1.refs_3_
  58.7 0.0 copy-start.1
  58.7 40.0 %window_attention.3 = (bf16[8,2,64,128]{3,2,1,0:T(8,128)(2,1)S(1)}, bf16[1024,256]{1,0:T(8,128)(2,1)}) custom-call(bf16[2,512,1024]{2,1,0:T(8,128)(2,1)S(1)} %copy-done, f32[2,1024]{1,0:T(2,128)S(1)} %copy-done.4, bf16[2,256,1024]{2,1,0:T(8,128)(2,1)S(1)} %collective-permute-done.refs_2_, bf16[256,1024]{1,0:T(8,128)(2,1)S(1)} %collective-permute-done.1.refs_3_, ...), custom_call_target="tpu_custom_call" | custom-call | flops 6442450944 | bytes 8388608 | tf_op jit(solution)/shard_map/window_attention/pallas_call | solution.py:304
  98.7 13.8 %all_to_all.15.gathered = bf16[8,2,64,128]{3,2,1,0:T(8,128)(2,1)S(1)} all-to-all(bf16[8,2,64,128]{3,2,1,0:T(8,128)(2,1)S(1)} %get-tuple-element.23), channel_id=1, replica_groups=mesh['ens'=8,'space'=16] {'ens'}, dimensions={0} | all-to-all | bytes 524288 | tf_op jit(solution)/shard_map/all_to_all | solution.py:441
  112.5 0.0 copy-done.1
  112.5 1.5 %fair_crps.1 = bf16[8,144,128]{2,1,0:T(8,128)(2,1)S(1)} custom-call(bf16[8,2,64,128]{3,2,1,0:T(8,128)(2,1)S(1)} %all_to_all.15.gathered, f32[512,128]{1,0:T(8,128)S(1)} %copy-done.1), custom_call_target="tpu_custom_call" | custom-call | tf_op jit(solution)/shard_map/fair_crps/pallas_call | solution.py:378
  114.0 10.6 %all_to_all.16.slopes = bf16[8,144,128]{2,1,0:T(8,128)(2,1)S(1)} all-to-all(bf16[8,144,128]{2,1,0:T(8,128)(2,1)S(1)} %fair_crps.1), channel_id=1, replica_groups=mesh['ens'=8,'space'=16] {'ens'}, dimensions={0} | all-to-all | bytes 589824 | tf_op jit(solution)/shard_map/all_to_all | solution.py:442
  124.6 0.6 broadcast_in_dim.3
  125.2 9.8 %all-to-all-start.2 = ((f32[16,1,128]{2,1,0:T(1,128)}), f32[16,1,128]{2,1,0:T(1,128)S(1)}, u32[]{:S(2)}, u32[]{:S(2)}) async-start(f32[16,1,128]{2,1,0:T(1,128)} %broadcast_in_dim.3), calls=%async_computation.2 | async-start | bytes 16384 | tf_op jit(solution)/shard_map/all_to_all | solution.py:445
  135.1 2.5 %state_grad.1 = bf16[2,512,1024]{2,1,0:T(8,128)(2,1)} custom-call(bf16[8,144,128]{2,1,0:T(8,128)(2,1)S(1)} %all_to_all.16.slopes, bf16[1024,128]{1,0:T(8,128)(2,1)S(1)} %copy-done.2), custom_call_target="tpu_custom_call" | custom-call | flops 268435456 | bytes 3145728 | tf_op jit(solution)/shard_map/state_grad/pallas_call | solution.py:405
  137.6 2.9 %all-to-all-done.2 = f32[16,1,128]{2,1,0:T(1,128)S(1)} async-done(((f32[16,1,128]{2,1,0:T(1,128)}), f32[16,1,128]{2,1,0:T(1,128)S(1)}, u32[]{:S(2)}, u32[]{:S(2)}) %all-to-all-start.2) | async-done | bytes 8224 | tf_op jit(solution)/shard_map/all_to_all | solution.py:445
  140.5 0.6 reduce_sum.19
  (1 shorter events, 0.0 us)
Async XLA Ops:
  0.6 6.8 %copy-start = (bf16[2,512,1024]{2,1,0:T(8,128)(2,1)S(1)}, bf16[2,512,1024]{2,1,0:T(8,128)(2,1)}, u32[]{:S(2)}) copy-start(bf16[2,512,1024]{2,1,0:T(8,128)(2,1)} %refs_0_.3) | copy-start | bytes 6291460
  2.2 16.2 %collective-permute-start = (bf16[2,256,1024]{2,1,0:T(8,128)(2,1)S(1)}, bf16[2,256,1024]{2,1,0:T(8,128)(2,1)S(1)}, u32[]{:S(2)}, u32[]{:S(2)}) collective-permute-start(bf16[2,256,1024]{2,1,0:T(8,128)(2,1)S(1)} %get-tuple-element.13), channel_id=1, source_target_pairs={{0,1},{2,3},{4,5},{6,7},{8,9},{10,11},{12,13},{14,15},{1,0},{3,2},... | collective-permute-start | bytes 3145736 | tf_op jit(solution)/shard_map/ppermute | solution.py:430
  3.7 14.8 %copy-start.2 = (bf16[1024,128]{1,0:T(8,128)(2,1)S(1)}, bf16[1024,128]{1,0:T(8,128)(2,1)}, u32[]{:S(2)}) copy-start(bf16[1024,128]{1,0:T(8,128)(2,1)} %w_decode.1) | copy-start | bytes 786436
  3.7 14.8 %copy-start.3 = (bf16[1024,1024]{1,0:T(8,128)(2,1)S(1)}, bf16[1024,1024]{1,0:T(8,128)(2,1)}, u32[]{:S(2)}) copy-start(bf16[1024,1024]{1,0:T(8,128)(2,1)} %refs_9_.3) | copy-start | bytes 6291460
  3.7 14.8 %copy-start.4 = (f32[2,1024]{1,0:T(2,128)S(1)}, f32[2,1024]{1,0:T(2,128)}, u32[]{:S(2)}) copy-start(f32[2,1024]{1,0:T(2,128)} %refs_1_.3) | copy-start | bytes 24580
  3.7 14.7 %collective-permute-start.2 = (bf16[256,1024]{1,0:T(8,128)(2,1)S(1)}, bf16[256,1024]{1,0:T(8,128)(2,1)S(1)}, u32[]{:S(2)}, u32[]{:S(2)}) collective-permute-start(bf16[256,1024]{1,0:T(8,128)(2,1)S(1)} %get-tuple-element.20), channel_id=1, source_target_pairs={{1,2},{3,4},{5,6},{7,8},{9,10},{11,12},{13,14},{2,1},{4,3},{6,5},{... | collective-permute-start | bytes 1572872 | tf_op jit(solution)/shard_map/ppermute | solution.py:429
  16.3 42.4 %collective-permute-start.1 = (bf16[256,1024]{1,0:T(8,128)(2,1)S(1)}, bf16[256,1024]{1,0:T(8,128)(2,1)S(1)}, u32[]{:S(2)}, u32[]{:S(2)}) collective-permute-start(bf16[256,1024]{1,0:T(8,128)(2,1)S(1)} %bitcast.2), channel_id=1, source_target_pairs={{1,2},{3,4},{5,6},{7,8},{9,10},{11,12},{13,14},{2,1},{4,3},{6,5},{... | collective-permute-start | bytes 1572872 | tf_op jit(solution)/shard_map/ppermute | solution.py:434
  58.7 53.9 %copy-start.1 = (f32[512,128]{1,0:T(8,128)S(1)}, f32[512,128]{1,0:T(8,128)}, u32[]{:S(2)}) copy-start(f32[512,128]{1,0:T(8,128)} %target.1) | copy-start | bytes 786436
  125.2 15.3 %all-to-all-start.2 = ((f32[16,1,128]{2,1,0:T(1,128)}), f32[16,1,128]{2,1,0:T(1,128)S(1)}, u32[]{:S(2)}, u32[]{:S(2)}) async-start(f32[16,1,128]{2,1,0:T(1,128)} %broadcast_in_dim.3), calls=%async_computation.2 | async-start | bytes 16384 | tf_op jit(solution)/shard_map/all_to_all | solution.py:445

commit v3 on v2

--- a/solution.py
+++ b/solution.py
@@ -12,7 +12,6 @@
 WIN = 256
 SMOOTH = 0.25
 EPS = 1e-5
-LOG2E = math.log2(math.e)
 SUB = 128
 UNROLL = 4
 TAIL = 16
@@ -40,15 +39,17 @@
     return parts
 
 
-def edges_kernel(states, far, near, sems):
+def edges_kernel(states, noise, w_query, far, near, shift, held_query, sems):
     rows = states.shape[1]
     even = lax.axis_index("space") % 2 == 0
     first, last = pl.ds(0, WIN), pl.ds(rows - WIN, WIN)
 
     def move(out, back):
         copies = [
-            pltpu.make_async_copy(states.at[0, out], far, sems.at[0]),
+            pltpu.make_async_copy(states.at[:, out], far, sems.at[0]),
             pltpu.make_async_copy(states.at[:, back], near, sems.at[1]),
+            pltpu.make_async_copy(noise, shift, sems.at[2]),
+            pltpu.make_async_copy(w_query, held_query, sems.at[3]),
         ]
         for copy in copies:
             copy.start()
@@ -64,52 +65,47 @@
         move(last, first)
 
 
-def edges(states):
+def edges(states, noise, w_query):
     members, _, width = states.shape
     return pl.pallas_call(
         edges_kernel,
         out_shape=[
-            jax.ShapeDtypeStruct((WIN, width), BF),
             jax.ShapeDtypeStruct((members, WIN, width), BF),
+            jax.ShapeDtypeStruct((members, WIN, width), BF),
+            pltpu.VMEM(noise.shape, F32),
+            pltpu.VMEM(w_query.shape, BF),
         ],
-        in_specs=[HBM],
-        out_specs=[VMEM] * 2,
-        scratch_shapes=[pltpu.SemaphoreType.DMA((2,))],
+        in_specs=[HBM] * 3,
+        out_specs=[VMEM] * 4,
+        scratch_shapes=[pltpu.SemaphoreType.DMA((4,))],
         compiler_params=params(4),
         name="edges",
-    )(pltpu.with_memory_space_constraint(states, pltpu.HBM))
+    )(*[pltpu.with_memory_space_constraint(x, pltpu.HBM) for x in (states, noise, w_query)])
 
 
 def qkv_kernel(
-    states, noise, w_query, w_key, w_value, query, keys, values, far, held_key, held_value,
-    norm, shift, held_query, sems,
+    states, noise, w_query, w_key, w_value, query, keys, values, held_key, held_value,
+    norm, sems,
 ):
     members, rows, width = states.shape
-    even = lax.axis_index("space") % 2 == 0
     scale = 1.0 / math.sqrt(width // HEADS)
     step = 256
     pieces = [(m, pl.ds(i * step, step)) for m in range(members) for i in range(rows // step)]
-    moves = [(noise, shift), (w_query, held_query), (w_key, held_key), (w_value, held_value)]
+    moves = [(w_key, held_key), (w_value, held_value)]
     copies = [pltpu.make_async_copy(a, b, sems.at[i]) for i, (a, b) in enumerate(moves)]
-    copies[0].start()
-    copies[1].start()
-    copies[0].wait()
+    for copy in copies:
+        copy.start()
     for m, at in pieces[:1]:
-        norm[m, at] = normed(states[m, at], shift[m : m + 1])
-    copies[1].wait()
-    copies[2].start()
-    copies[3].start()
+        norm[m, at] = normed(states[m, at], noise[m : m + 1])
     for i, (m, at) in enumerate(pieces):
         x = norm[m, at]
-        query[m, at] = (jnp.dot(x, held_query[...], preferred_element_type=F32) * scale).astype(BF)
+        query[m, at] = (jnp.dot(x, w_query[...], preferred_element_type=F32) * scale).astype(BF)
         for later, part in pieces[i + 1 : i + 2]:
-            norm[later, part] = normed(states[later, part], shift[later : later + 1])
-    for m in range(1, members):
-        far[m - 1] = jnp.where(even, states[m, :WIN], states[m, rows - WIN :])
-    copies[2].wait()
+            norm[later, part] = normed(states[later, part], noise[later : later + 1])
+    copies[0].wait()
     for m, at in pieces:
         keys[m, at] = jnp.dot(norm[m, at], held_key[...], preferred_element_type=F32).astype(BF)
-    copies[3].wait()
+    copies[1].wait()
     for m, at in pieces:
         values[m, at] = jnp.dot(norm[m, at], held_value[...], preferred_element_type=F32).astype(BF)
 
@@ -119,27 +115,24 @@
     return pl.pallas_call(
         qkv_kernel,
         out_shape=[jax.ShapeDtypeStruct(states.shape, BF)] * 3
-        + [jax.ShapeDtypeStruct((members - 1, WIN, width), BF)]
         + [pltpu.VMEM(x.shape, BF) for x in (w_key, w_value)],
-        in_specs=[VMEM] + [HBM] * 4,
-        out_specs=[VMEM] * 6,
+        in_specs=[VMEM] * 3 + [HBM] * 2,
+        out_specs=[VMEM] * 5,
         scratch_shapes=[
             pltpu.VMEM(states.shape, BF),
-            pltpu.VMEM(noise.shape, F32),
-            pltpu.VMEM(w_query.shape, BF),
-            pltpu.SemaphoreType.DMA((4,)),
+            pltpu.SemaphoreType.DMA((2,)),
         ],
         compiler_params=params(20),
         cost_estimate=pl.CostEstimate(
             flops=6 * members * rows * width * width, bytes_accessed=8 * 2**20, transcendentals=0
         ),
         name="own_qkv",
-    )(states, *[pltpu.with_memory_space_constraint(x, pltpu.HBM) for x in (noise, w_query, w_key, w_value)])
+    )(states, noise, w_query, *[pltpu.with_memory_space_constraint(x, pltpu.HBM) for x in (w_key, w_value)])
 
 
 def attend_kernel(
     m, states, noise, inner, outer, query, keys, values, w_key, w_value, w_out, w_decode, earlier,
-    forecast, w_both, halo_k, halo_v, kk, vv, mixed, bad,
+    w_both, forecast, halo_k, halo_v, kk, vv, mixed, bad, base,
 ):
     members, rows, width = states.shape
     pairs = width // SUB
@@ -205,7 +198,7 @@
         )
         parts = []
         for j in range(2 * span):
-            parts.append(jnp.exp2(masked(s[:, j * SUB : (j + 1) * SUB] * LOG2E, j // 2)).astype(BF))
+            parts.append(jnp.exp(masked(s[:, j * SUB : (j + 1) * SUB], j // 2)).astype(BF))
         o = jnp.dot(jnp.concatenate(parts, axis=1), vv[u, at], preferred_element_type=F32)
         norms = o[:, SUB:]
         mixed[a * SUB : (a + 1) * SUB, c] = (o[:, :SUB] / norms).astype(BF)
@@ -222,13 +215,13 @@
                 key = source(m, keys, halo_k, j, c)
                 own = jnp.where(mine, q, zero)
                 s = lax.dot_general(own, key, NT, preferred_element_type=F32)
-                s = masked(s * LOG2E, j - a)
+                s = masked(s, j - a)
                 if outside(j):
                     s = jnp.where(absent(j), -1e30, s)
                 scores.append(s)
                 vals.append(source(m, values, halo_v, j, c))
             s = jnp.concatenate(scores, axis=1)
-            p = jnp.exp2(s - jnp.max(s, axis=-1, keepdims=True))
+            p = jnp.exp(s - jnp.max(s, axis=-1, keepdims=True))
             norms = jnp.sum(p, axis=-1, keepdims=True)
             outs.append(
                 jnp.dot(
@@ -252,9 +245,16 @@
         product = jnp.dot(w_out[...], w_decode[...], preferred_element_type=F32)
         w_both[:, :lanes], w_both[:, lanes:] = split(product, 2)
     else:
-        w_both[...] = earlier[0][...]
         for i in range(m):
-            forecast[:, i] = earlier[1][:, i]
+            forecast[:, i] = earlier[:, i]
+
+    constant = jnp.dot(
+        jnp.concatenate([jnp.broadcast_to(x, (8, width)) for x in split(shift, 3)], axis=0),
+        w_decode[...],
+        preferred_element_type=F32,
+    )
+    constant = constant[0:1] + constant[8:9] + constant[16:17]
+    base[...] = jnp.dot(states[m], w_decode[...], preferred_element_type=F32) + constant
 
     def heads(i, _):
         for u in range(UNROLL):
@@ -264,7 +264,17 @@
                 block(m, u, i * UNROLL + u, a)
         return 0
 
+    def finish():
+        share = rows // forecast.shape[0]
+        for i in range(rows // 256):
+            at = slice(i * 256, (i + 1) * 256)
+            out = jnp.dot(mixed[at], w_both[...], preferred_element_type=F32)
+            out = out[:, :lanes] + out[:, lanes:] + base[at]
+            each = 256 // share
+            forecast[i * each : (i + 1) * each, m] = out.astype(BF).reshape(each, share, -1)
+
     lax.fori_loop(0, pairs // UNROLL, heads, 0)
+    finish()
 
     @pl.when(jnp.max(bad[...]) > 0.0)
     def _():
@@ -274,41 +284,30 @@
             return 0
 
         lax.fori_loop(0, pairs, again, 0)
-
-    constant = jnp.dot(
-        jnp.concatenate([jnp.broadcast_to(x, (8, width)) for x in split(shift, 3)], axis=0),
-        w_decode[...],
-        preferred_element_type=F32,
-    )
-    constant = constant[0:1] + constant[8:9] + constant[16:17]
-    for i in range(rows // 256):
-        at = slice(i * 256, (i + 1) * 256)
-        out = jnp.dot(mixed[at], w_both[...], preferred_element_type=F32)
-        out = out[:, :lanes] + out[:, lanes:] + constant
-        out = out + jnp.dot(states[m, at], w_decode[...], preferred_element_type=F32)
-        share = rows // forecast.shape[0]
-        each = 256 // share
-        forecast[i * each : (i + 1) * each, m] = out.astype(BF).reshape(each, share, -1)
+        finish()
 
 
 def attend(m, states, noise, inner, outer, query, keys, values, w_key, w_value, w_out, w_decode, shares, earlier):
     members, rows, width = states.shape
     held = 2 * WIN + rows
     lanes = w_decode.shape[1]
+    ready = jax.ShapeDtypeStruct((shares, members, rows // shares, lanes), BF)
+    product = jax.ShapeDtypeStruct((width, 2 * lanes), BF)
     taken = [] if earlier is None else list(earlier)
 
     def kernel(*refs):
         ins, rest = refs[:11], refs[11:]
-        attend_kernel(m, *ins, rest[: len(taken)], *rest[len(taken) :])
+        if taken:
+            before, w_both, forecast = rest[:3]
+        else:
+            before, w_both, forecast = None, rest[0], rest[1]
+        attend_kernel(m, *ins, before, w_both, forecast, *rest[2 + len(taken) // 2 :])
 
     return pl.pallas_call(
         kernel,
-        out_shape=[
-            jax.ShapeDtypeStruct((shares, members, rows // shares, lanes), BF),
-            jax.ShapeDtypeStruct((width, 2 * lanes), BF),
-        ],
+        out_shape=[ready] if taken else [product, ready],
         in_specs=[VMEM] * (11 + len(taken)),
-        out_specs=[VMEM] * 2,
+        out_specs=[VMEM] * (1 if taken else 2),
         scratch_shapes=[
             pltpu.VMEM((2 * WIN, width), BF),
             pltpu.VMEM((2 * WIN, width), BF),
@@ -316,6 +315,7 @@
             pltpu.VMEM((UNROLL, 2 * held, 2 * SUB), BF),
             pltpu.VMEM((rows, width), BF),
             pltpu.VMEM((SUB, SUB), F32),
+            pltpu.VMEM((rows, lanes), F32),
         ],
         compiler_params=params(24),
         cost_estimate=pl.CostEstimate(
@@ -327,7 +327,7 @@
     )(states, noise, inner, outer, query, keys, values, w_key, w_value, w_out, w_decode, *taken)
 
 
-def crps_kernel(gathered, target, grad):
+def crps_kernel(count, gathered, target, grad):
     groups, local, share, lanes = gathered.shape
     members = groups * local
     first = lax.axis_index("ens") * share
@@ -364,7 +364,7 @@
         return total
 
     total = lax.fori_loop(0, share // 16, piece, jnp.zeros((8, lanes), F32))
-    terms = split(jnp.sum(total, axis=0, keepdims=True), 3)
+    terms = split(jnp.sum(total, axis=0, keepdims=True) * (1.0 / count), 3)
     row = lax.broadcasted_iota(jnp.int32, (TAIL, lanes), 0)
     tail = jnp.zeros((TAIL, lanes), F32)
     for i, term in enumerate(terms):
@@ -373,10 +373,10 @@
         grad[i, local * share :] = tail.astype(BF)
 
 
-def crps(gathered, target):
+def crps(gathered, target, count):
     groups, local, share, lanes = gathered.shape
     return pl.pallas_call(
-        crps_kernel,
+        functools.partial(crps_kernel, count),
         out_shape=jax.ShapeDtypeStruct((groups, local * share + TAIL, lanes), BF),
         in_specs=[VMEM, VMEM],
         out_specs=VMEM,
@@ -425,26 +425,27 @@
     cross = [(i, i + 1) for i in range(1, space - 1, 2)]
     chip = [(i, i + 1) for i in range(0, space, 2)]
     both = lambda pairs: pairs + [(j, i) for i, j in pairs]
-    far, near = edges(states)
-    outer = [lax.ppermute(far, "space", both(cross))]
+    far, near, member_noise, w_query = edges(states, member_noise, w_query)
+    outer = [lax.ppermute(far[m], "space", both(cross)) for m in range(members)]
     inner = lax.ppermute(near, "space", both(chip))
-    query, keys, values, far, w_key, w_value = qkv(
+    query, keys, values, w_key, w_value = qkv(
         states, member_noise, w_query, w_key, w_value
     )
-    outer += [lax.ppermute(far[m], "space", both(cross)) for m in range(members - 1)]
-    done = None
+    taken = None
     for m in range(members):
         done = attend(
             m, states, member_noise, inner, outer[m], query, keys, values,
-            w_key, w_value, w_out, w_decode, ens, done and (done[1], done[0]),
+            w_key, w_value, w_out, w_decode, ens, taken,
         )
-    gathered = lax.all_to_all(done[0], "ens", 0, 0)
-    slopes = lax.all_to_all(crps(gathered, target), "ens", 0, 0)
+        product = product if m else done[0]
+        taken = (done[-1], product)
+    gathered = lax.all_to_all(done[-1], "ens", 0, 0)
+    count = members * ens * rows * space * w_decode.shape[1]
+    slopes = lax.all_to_all(crps(gathered, target, count), "ens", 0, 0)
     held = slopes.shape[1] - TAIL
     part = jnp.sum(slopes[:, held : held + 3].astype(F32), axis=(0, 1))
     parts = lax.all_to_all(jnp.broadcast_to(part, (space, 1, part.shape[0])), "space", 0, 0)
-    loss = jnp.sum(parts) / (members * ens * rows * space * w_decode.shape[1])
-    return back(slopes, w_decode, members), loss
+    return back(slopes, w_decode, members), jnp.sum(parts)
 
 
 def solution(mesh):

time: 143 us -> 141 us (0.986)
  between operations: 2.52 us -> 0.76 us
    pallas_call x4, Pallas kernels: 83.2 us -> 84.9 us  [the longest x2 81.1 us: attend(): pl.pallas_call(kernel, out_shape=[ready] if taken else [product, ready],...]
    pallas_call x1, Pallas kernels: 8.84 us -> 7.32 us  [qkv(): pl.pallas_call(qkv_kernel, out_shape=[jax.ShapeDtypeStruct(states.shape,...]
where the time goes in v3:
time: 141 us
  Pallas kernels  94.8 us (67%)
  blocking collectives  24.4 us (17%)
  starting transfers between devices  17 us (12%)
  waiting for transfers between devices  2.95 us (2%)
    pallas_call x2, Pallas kernels, attend(): pl.pallas_call(kernel, out_shape=[ready] if taken else [product, ready],...  81.1 us
    all_to_all x1, blocking collectives, body(): gathered = lax.all_to_all(done[-1], 'ens', 0, 0)  13.8 us
    all_to_all x1, blocking collectives, body(): slopes = lax.all_to_all(crps(gathered, target, count), 'ens', 0, 0)  10.6 us
    all_to_all x1, starting transfers between devices, body(): lax.all_to_all(jnp.broadcast_to(part, (space, 1, part.shape[0])), 'space'...  9.89 us
    pallas_call x1, Pallas kernels, qkv(): pl.pallas_call(qkv_kernel, out_shape=[jax.ShapeDtypeStruct(states.shape,...  7.32 us
    ppermute x2, starting transfers between devices, body(): outer = [lax.ppermute(far[m], 'space', both(cross)) for m in range(members)]  5.59 us
    all_to_all x1, waiting for transfers between devices, body(): lax.all_to_all(jnp.broadcast_to(part, (space, 1, part.shape[0])), 'space'...  2.94 us
  transfers between devices with their start and end apart: 4, of which 1 were waited for; matrix products, arithmetic and copies ran while one was open for 0% of the time, Pallas kernels for 36%

profile of v3, /device:TPU:1, one launch (start us, length us, event | category | flops | bytes accessed | tf_op | source)
XLA Modules:
  0.0 141.2 jit_solution(1692002183735092928)
XLA Ops:
  0.6 2.3 %edges.1 = (bf16[2,256,1024]{2,1,0:T(8,128)(2,1)S(1)}, bf16[2,256,1024]{2,1,0:T(8,128)(2,1)S(1)}, f32[2,1024]{1,0:T(2,128)S(1)}, bf16[1024,1024]{1,0:T(8,128)(2,1)S(1)}) custom-call(bf16[2,512,1024]{2,1,0:T(8,128)(2,1)} %refs_0_.3, f32[2,1024]{1,0:T(2,128)} %noise.1, bf16[1024,1024]{1,0:T(8,128)(2,1)} %w_query.1), custom_call_target="tpu_custom_call" | custom-call | tf_op jit(solution)/shard_map/edges/pallas_call | solution.py:70
  2.9 0.0 copy-start
  3.0 1.5 %collective-permute-start = (bf16[2,256,1024]{2,1,0:T(8,128)(2,1)S(1)}, bf16[2,256,1024]{2,1,0:T(8,128)(2,1)S(1)}, u32[]{:S(2)}, u32[]{:S(2)}) collective-permute-start(bf16[2,256,1024]{2,1,0:T(8,128)(2,1)S(1)} %get-tuple-element.14), channel_id=1, source_target_pairs={{0,1},{2,3},{4,5},{6,7},{8,9},{10,11},{12,13},{14,15},{1,0},{3,2},... | collective-permute-start | bytes 3145736 | tf_op jit(solution)/shard_map/ppermute | solution.py:430
  4.5 0.1 slice_bitcast_fusion
  4.5 3.7 %collective-permute-start.2 = (bf16[256,1024]{1,0:T(8,128)(2,1)S(1)}, bf16[256,1024]{1,0:T(8,128)(2,1)S(1)}, u32[]{:S(2)}, u32[]{:S(2)}) collective-permute-start(bf16[256,1024]{1,0:T(8,128)(2,1)S(1)} %get-tuple-element.24), channel_id=1, source_target_pairs={{1,2},{3,4},{5,6},{7,8},{9,10},{11,12},{13,14},{2,1},{4,3},{6,5},{... | collective-permute-start | bytes 1572872 | tf_op jit(solution)/shard_map/ppermute | solution.py:429
  8.2 1.9 %collective-permute-start.1 = (bf16[256,1024]{1,0:T(8,128)(2,1)S(1)}, bf16[256,1024]{1,0:T(8,128)(2,1)S(1)}, u32[]{:S(2)}, u32[]{:S(2)}) collective-permute-start(bf16[256,1024]{1,0:T(8,128)(2,1)S(1)} %get-tuple-element.25), channel_id=1, source_target_pairs={{1,2},{3,4},{5,6},{7,8},{9,10},{11,12},{13,14},{2,1},{4,3},{6,5},{... | collective-permute-start | bytes 1572872 | tf_op jit(solution)/shard_map/ppermute | solution.py:429
  10.1 0.0 copy-done
  10.1 0.0 copy-start.2
  10.1 0.0 copy-start.3
  10.2 7.3 %own_qkv.1 = (bf16[2,512,1024]{2,1,0:T(8,128)(2,1)S(1)}, bf16[2,512,1024]{2,1,0:T(8,128)(2,1)S(1)}, bf16[2,512,1024]{2,1,0:T(8,128)(2,1)S(1)}, bf16[1024,1024]{1,0:T(8,128)(2,1)S(1)}, bf16[1024,1024]{1,0:T(8,128)(2,1)S(1)}) custom-call(bf16[2,512,1024]{2,1,0:T(8,128)(2,1)S(1)} %copy-done, f32[2,1024]{1,0:T(2,128)S(1)} %get-tuple-element.13.noise.refs_1_, ...), custom_call_target="tpu_custom_call" | custom-call | flops 6442450944 | bytes 8388608 | tf_op jit(solution)/shard_map/own_qkv/pallas_call | solution.py:115
  17.5 0.0 collective-permute-done.2.refs_3_
  17.5 0.0 collective-permute-done.refs_2_
  17.5 0.0 copy-done.2
  17.5 0.0 copy-done.3
  17.5 40.8 %window_attention.2 = (bf16[1024,256]{1,0:T(8,128)(2,1)S(1)}, bf16[8,2,64,128]{3,2,1,0:T(8,128)(2,1)S(1)}) custom-call(bf16[2,512,1024]{2,1,0:T(8,128)(2,1)S(1)} %copy-done, f32[2,1024]{1,0:T(2,128)S(1)} %get-tuple-element.13.noise.refs_1_, bf16[2,256,1024]{2,1,0:T(8,128)(2,1)S(1)} %collective-permute-done.refs_2_, ...), custom_call_target="tpu_custom_call" | custom-call | flops 6442450944 | bytes 8388608 | tf_op jit(solution)/shard_map/window_attention/pallas_call | solution.py:306
  58.3 0.0 collective-permute-done.1.refs_3_
  58.3 0.0 copy-start.1
  58.3 40.3 %window_attention.3 = bf16[8,2,64,128]{3,2,1,0:T(8,128)(2,1)S(1)} custom-call(bf16[2,512,1024]{2,1,0:T(8,128)(2,1)S(1)} %copy-done, f32[2,1024]{1,0:T(2,128)S(1)} %get-tuple-element.13.noise.refs_1_, bf16[2,256,1024]{2,1,0:T(8,128)(2,1)S(1)} %collective-permute-done.refs_2_, bf16[256,1024]{1,0:T(8,128)(2,1)S(1)} %collective-permute-done.1.refs_3_, ...), custom_call_target="tpu_custom_call" | custom-call | flops 6442450944 | bytes 8388608 | tf_op jit(solution)/shard_map/window_attention/pallas_call | solution.py:306
  98.7 13.8 %all_to_all.15.gathered = bf16[8,2,64,128]{3,2,1,0:T(8,128)(2,1)S(1)} all-to-all(bf16[8,2,64,128]{3,2,1,0:T(8,128)(2,1)S(1)} %window_attention.3), channel_id=1, replica_groups=mesh['ens'=8,'space'=16] {'ens'}, dimensions={0} | all-to-all | bytes 524288 | tf_op jit(solution)/shard_map/all_to_all | solution.py:442
  112.5 0.0 copy-done.1
  112.5 1.5 %fair_crps.1 = bf16[8,144,128]{2,1,0:T(8,128)(2,1)S(1)} custom-call(bf16[8,2,64,128]{3,2,1,0:T(8,128)(2,1)S(1)} %all_to_all.15.gathered, f32[512,128]{1,0:T(8,128)S(1)} %copy-done.1), custom_call_target="tpu_custom_call" | custom-call | tf_op jit(solution)/shard_map/fair_crps/pallas_call | solution.py:378
  114.0 10.6 %all_to_all.16.slopes = bf16[8,144,128]{2,1,0:T(8,128)(2,1)S(1)} all-to-all(bf16[8,144,128]{2,1,0:T(8,128)(2,1)S(1)} %fair_crps.1), channel_id=1, replica_groups=mesh['ens'=8,'space'=16] {'ens'}, dimensions={0} | all-to-all | bytes 589824 | tf_op jit(solution)/shard_map/all_to_all | solution.py:444
  124.6 0.6 broadcast_in_dim.3
  125.2 9.9 %all-to-all-start.2 = ((f32[16,1,128]{2,1,0:T(1,128)}), f32[16,1,128]{2,1,0:T(1,128)S(1)}, u32[]{:S(2)}, u32[]{:S(2)}) async-start(f32[16,1,128]{2,1,0:T(1,128)} %broadcast_in_dim.3), calls=%async_computation.2 | async-start | bytes 16384 | tf_op jit(solution)/shard_map/all_to_all | solution.py:447
  135.1 2.5 %state_grad.1 = bf16[2,512,1024]{2,1,0:T(8,128)(2,1)} custom-call(bf16[8,144,128]{2,1,0:T(8,128)(2,1)S(1)} %all_to_all.16.slopes, bf16[1024,128]{1,0:T(8,128)(2,1)S(1)} %copy-done.2), custom_call_target="tpu_custom_call" | custom-call | flops 268435456 | bytes 3145728 | tf_op jit(solution)/shard_map/state_grad/pallas_call | solution.py:405
  137.6 2.9 %all-to-all-done.2 = f32[16,1,128]{2,1,0:T(1,128)S(1)} async-done(((f32[16,1,128]{2,1,0:T(1,128)}), f32[16,1,128]{2,1,0:T(1,128)S(1)}, u32[]{:S(2)}, u32[]{:S(2)}) %all-to-all-start.2) | async-done | bytes 8224 | tf_op jit(solution)/shard_map/all_to_all | solution.py:447
  140.6 0.6 reduce_sum.19
  (1 shorter events, 0.0 us)
Async XLA Ops:
  2.9 7.2 %copy-start = (bf16[2,512,1024]{2,1,0:T(8,128)(2,1)S(1)}, bf16[2,512,1024]{2,1,0:T(8,128)(2,1)}, u32[]{:S(2)}) copy-start(bf16[2,512,1024]{2,1,0:T(8,128)(2,1)} %refs_0_.3) | copy-start | bytes 6291460
  3.0 14.5 %collective-permute-start = (bf16[2,256,1024]{2,1,0:T(8,128)(2,1)S(1)}, bf16[2,256,1024]{2,1,0:T(8,128)(2,1)S(1)}, u32[]{:S(2)}, u32[]{:S(2)}) collective-permute-start(bf16[2,256,1024]{2,1,0:T(8,128)(2,1)S(1)} %get-tuple-element.14), channel_id=1, source_target_pairs={{0,1},{2,3},{4,5},{6,7},{8,9},{10,11},{12,13},{14,15},{1,0},{3,2},... | collective-permute-start | bytes 3145736 | tf_op jit(solution)/shard_map/ppermute | solution.py:430
  4.5 13.0 %collective-permute-start.2 = (bf16[256,1024]{1,0:T(8,128)(2,1)S(1)}, bf16[256,1024]{1,0:T(8,128)(2,1)S(1)}, u32[]{:S(2)}, u32[]{:S(2)}) collective-permute-start(bf16[256,1024]{1,0:T(8,128)(2,1)S(1)} %get-tuple-element.24), channel_id=1, source_target_pairs={{1,2},{3,4},{5,6},{7,8},{9,10},{11,12},{13,14},{2,1},{4,3},{6,5},{... | collective-permute-start | bytes 1572872 | tf_op jit(solution)/shard_map/ppermute | solution.py:429
  8.2 50.1 %collective-permute-start.1 = (bf16[256,1024]{1,0:T(8,128)(2,1)S(1)}, bf16[256,1024]{1,0:T(8,128)(2,1)S(1)}, u32[]{:S(2)}, u32[]{:S(2)}) collective-permute-start(bf16[256,1024]{1,0:T(8,128)(2,1)S(1)} %get-tuple-element.25), channel_id=1, source_target_pairs={{1,2},{3,4},{5,6},{7,8},{9,10},{11,12},{13,14},{2,1},{4,3},{6,5},{... | collective-permute-start | bytes 1572872 | tf_op jit(solution)/shard_map/ppermute | solution.py:429
  10.1 7.4 %copy-start.2 = (bf16[1024,128]{1,0:T(8,128)(2,1)S(1)}, bf16[1024,128]{1,0:T(8,128)(2,1)}, u32[]{:S(2)}) copy-start(bf16[1024,128]{1,0:T(8,128)(2,1)} %w_decode.1) | copy-start | bytes 786436
  10.1 7.4 %copy-start.3 = (bf16[1024,1024]{1,0:T(8,128)(2,1)S(1)}, bf16[1024,1024]{1,0:T(8,128)(2,1)}, u32[]{:S(2)}) copy-start(bf16[1024,1024]{1,0:T(8,128)(2,1)} %refs_9_.3) | copy-start | bytes 6291460
  58.3 54.2 %copy-start.1 = (f32[512,128]{1,0:T(8,128)S(1)}, f32[512,128]{1,0:T(8,128)}, u32[]{:S(2)}) copy-start(f32[512,128]{1,0:T(8,128)} %target.1) | copy-start | bytes 786436
  125.2 15.4 %all-to-all-start.2 = ((f32[16,1,128]{2,1,0:T(1,128)}), f32[16,1,128]{2,1,0:T(1,128)S(1)}, u32[]{:S(2)}, u32[]{:S(2)}) async-start(f32[16,1,128]{2,1,0:T(1,128)} %broadcast_in_dim.3), calls=%async_computation.2 | async-start | bytes 16384 | tf_op jit(solution)/shard_map/all_to_all | solution.py:447

commit v4 on v3

--- a/solution.py
+++ b/solution.py
@@ -1,5 +1,6 @@
 import functools
 import math
+import types
 
 import jax
 import jax.numpy as jnp
@@ -13,7 +14,9 @@
 SMOOTH = 0.25
 EPS = 1e-5
 SUB = 128
-UNROLL = 4
+UNROLL = {"own": 8, "halo": 8, "all": 8}
+AHEAD = {"own": 1, "halo": 2, "all": 0}
+CHUNK = {"own": 4, "halo": 2, "all": 5}
 TAIL = 16
 LOW, HIGH = 2.0**-80, 2.0**100
 BF, F32 = jnp.bfloat16, jnp.float32
@@ -130,16 +133,20 @@
     )(states, noise, w_query, *[pltpu.with_memory_space_constraint(x, pltpu.HBM) for x in (w_key, w_value)])
 
 
-def attend_kernel(
-    m, states, noise, inner, outer, query, keys, values, w_key, w_value, w_out, w_decode, earlier,
-    w_both, forecast, halo_k, halo_v, kk, vv, mixed, bad, base,
-):
-    members, rows, width = states.shape
+def attend_kernel(kind, m, names, *refs):
+    r = types.SimpleNamespace(**dict(zip(names, refs)))
+    query, keys, values = r.query, r.keys, r.values
+    kk, vv = r.kk, r.vv
+    unroll = UNROLL[kind]
+    members, rows, width = query.shape
     pairs = width // SUB
     subs = rows // SUB
     pad = WIN // SUB
     span = 2 * pad + 1
     total = subs + 2 * pad
+    inside = [j for j in range(total) if pad <= j < pad + subs]
+    held = {"own": inside, "halo": [j for j in range(total) if j not in inside]}
+    held = held.get(kind, list(range(total)))
     lane = lax.broadcasted_iota(jnp.int32, (SUB, SUB), 1)
     row = lax.broadcasted_iota(jnp.int32, (SUB, SUB), 0)
     left = lane < SUB // 2
@@ -154,12 +161,12 @@
         return starts if j < pad else ends
 
     def outside(j):
-        return j < pad or j >= pad + subs
-
-    for u in range(UNROLL):
-        for j in range(total):
+        return j not in inside
+
+    for u in range(unroll):
+        for n, j in enumerate(held):
             unit = jnp.where(absent(j), zero, one) if outside(j) else one
-            at = 2 * SUB * j
+            at = 2 * SUB * n
             vv[u, at : at + SUB, SUB:] = jnp.where(left, unit, zero)
             vv[u, at + SUB : at + 2 * SUB, SUB:] = jnp.where(left, zero, unit)
 
@@ -170,10 +177,12 @@
             return inner[m, (j - pad) * SUB : (j - pad + 1) * SUB, c]
         return halo[(j - subs) * SUB : (j - subs + 1) * SUB, c]
 
+    halo_k, halo_v = (None, None) if kind == "own" else (r.halo_k, r.halo_v)
+
     def pack(m, u, pair):
         c = pl.ds(pl.multiple_of(pair * SUB, SUB), SUB)
-        for j in range(total):
-            at = 2 * SUB * j
+        for n, j in enumerate(held):
+            at = 2 * SUB * n
             key = source(m, keys, halo_k, j, c)
             value = source(m, values, halo_v, j, c)
             if outside(j):
@@ -190,19 +199,39 @@
             return jnp.where(lane <= row, s, -1e30)
         return s
 
-    def block(m, u, pair, a):
+    def chunks(a):
+        window = [j for j in range(a, a + span) if j in held]
+        return [window[i : i + CHUNK[kind]] for i in range(0, len(window), CHUNK[kind])]
+
+    def packed(window):
+        first = held.index(window[0])
+        return slice(2 * SUB * first, 2 * SUB * (first + len(window)))
+
+    def weigh(m, u, pair, a, window):
         c = pl.ds(pl.multiple_of(pair * SUB, SUB), SUB)
-        at = slice(2 * SUB * a, 2 * SUB * (a + span))
-        s = lax.dot_general(
-            query[m, a * SUB : (a + 1) * SUB, c], kk[u, at], NT, preferred_element_type=F32
-        )
+        own = slice(a * SUB, (a + 1) * SUB)
+        at = packed(window)
+        s = lax.dot_general(query[m, own, c], kk[u, at], NT, preferred_element_type=F32)
         parts = []
-        for j in range(2 * span):
-            parts.append(jnp.exp(masked(s[:, j * SUB : (j + 1) * SUB], j // 2)).astype(BF))
-        o = jnp.dot(jnp.concatenate(parts, axis=1), vv[u, at], preferred_element_type=F32)
+        for n, j in enumerate(window):
+            for k in range(2 * n, 2 * n + 2):
+                parts.append(jnp.exp(masked(s[:, k * SUB : (k + 1) * SUB], j - a)).astype(BF))
+        return jnp.concatenate(parts, axis=1)
+
+    def mix(u, window, weights):
+        return jnp.dot(weights, vv[u, packed(window)], preferred_element_type=F32)
+
+    def store(pair, a, o):
+        c = pl.ds(pl.multiple_of(pair * SUB, SUB), SUB)
+        own = slice(a * SUB, (a + 1) * SUB)
+        if kind == "own":
+            r.partial[pair, own] = o
+            return
+        if kind == "halo":
+            o = o + r.partial[pair, own]
         norms = o[:, SUB:]
-        mixed[a * SUB : (a + 1) * SUB, c] = (o[:, :SUB] / norms).astype(BF)
-        bad[...] = jnp.where((norms > LOW) & (norms < HIGH), bad[...], 1.0)
+        r.mixed[own, c] = (o[:, :SUB] / norms).astype(BF)
+        r.bad[...] = jnp.where((norms > LOW) & (norms < HIGH), r.bad[...], 1.0)
 
     def safe_block(m, pair, a):
         c = pl.ds(pl.multiple_of(pair * SUB, SUB), SUB)
@@ -230,53 +259,68 @@
                     preferred_element_type=F32,
                 )
             )
-        mixed[a * SUB : (a + 1) * SUB, c] = jnp.where(left, outs[0], outs[1]).astype(BF)
-
-    shift = noise[m : m + 1]
+        r.mixed[a * SUB : (a + 1) * SUB, c] = jnp.where(left, outs[0], outs[1]).astype(BF)
+
+    def heads(i, _):
+        for u in range(unroll):
+            pack(m, u, i * unroll + u)
+        steps = [(u, a, w) for u in range(unroll) for a in range(subs) for w in chunks(a)]
+        ready, sums = [], {}
+        for n in range(len(steps) + AHEAD[kind]):
+            if n < len(steps):
+                u, a, window = steps[n]
+                ready.append(weigh(m, u, i * unroll + u, a, window))
+            if n >= AHEAD[kind]:
+                u, a, window = steps[n - AHEAD[kind]]
+                o = mix(u, window, ready[n - AHEAD[kind]])
+                o = sums[u, a] + o if (u, a) in sums else o
+                sums[u, a] = o
+                if window == chunks(a)[-1]:
+                    store(i * unroll + u, a, o)
+        return 0
+
+    shift = r.noise[m : m + 1]
+    if kind != "halo":
+        constant = jnp.dot(
+            jnp.concatenate([jnp.broadcast_to(x, (8, width)) for x in split(shift, 3)], axis=0),
+            r.w_decode[...],
+            preferred_element_type=F32,
+        )
+        constant = constant[0:1] + constant[8:9] + constant[16:17]
+        r.base[...] = constant + jnp.dot(
+            r.states[m], r.w_decode[...], preferred_element_type=F32
+        )
+    if kind == "own":
+        lanes = r.w_decode.shape[1]
+        product = jnp.dot(r.w_out[...], r.w_decode[...], preferred_element_type=F32)
+        r.w_both[:, :lanes], r.w_both[:, lanes:] = split(product, 2)
+        lax.fori_loop(0, pairs // unroll, heads, 0)
+        return
+
     for side in range(2):
-        x = normed(jnp.where(even == (side == 0), outer[...], inner[m]), shift)
+        x = normed(jnp.where(even == (side == 0), r.outer[m], r.inner[m]), shift)
         at = slice(side * WIN, (side + 1) * WIN)
-        halo_k[at] = jnp.dot(x, w_key[...], preferred_element_type=F32).astype(BF)
-        halo_v[at] = jnp.dot(x, w_value[...], preferred_element_type=F32).astype(BF)
-    bad[...] = jnp.zeros_like(bad)
-
-    lanes = w_decode.shape[1]
-    if m == 0:
-        product = jnp.dot(w_out[...], w_decode[...], preferred_element_type=F32)
-        w_both[:, :lanes], w_both[:, lanes:] = split(product, 2)
-    else:
-        for i in range(m):
-            forecast[:, i] = earlier[:, i]
-
-    constant = jnp.dot(
-        jnp.concatenate([jnp.broadcast_to(x, (8, width)) for x in split(shift, 3)], axis=0),
-        w_decode[...],
-        preferred_element_type=F32,
-    )
-    constant = constant[0:1] + constant[8:9] + constant[16:17]
-    base[...] = jnp.dot(states[m], w_decode[...], preferred_element_type=F32) + constant
-
-    def heads(i, _):
-        for u in range(UNROLL):
-            pack(m, u, i * UNROLL + u)
-        for u in range(UNROLL):
-            for a in range(subs):
-                block(m, u, i * UNROLL + u, a)
-        return 0
+        halo_k[at] = jnp.dot(x, r.w_key[...], preferred_element_type=F32).astype(BF)
+        halo_v[at] = jnp.dot(x, r.w_value[...], preferred_element_type=F32).astype(BF)
+    r.bad[...] = jnp.zeros_like(r.bad)
+    for i in range(m):
+        r.forecast[:, i] = r.earlier[:, i]
 
     def finish():
+        forecast = r.forecast
+        lanes = forecast.shape[3]
         share = rows // forecast.shape[0]
         for i in range(rows // 256):
             at = slice(i * 256, (i + 1) * 256)
-            out = jnp.dot(mixed[at], w_both[...], preferred_element_type=F32)
-            out = out[:, :lanes] + out[:, lanes:] + base[at]
+            out = jnp.dot(r.mixed[at], r.w_both[...], preferred_element_type=F32)
+            out = out[:, :lanes] + out[:, lanes:] + r.base[at]
             each = 256 // share
             forecast[i * each : (i + 1) * each, m] = out.astype(BF).reshape(each, share, -1)
 
-    lax.fori_loop(0, pairs // UNROLL, heads, 0)
+    lax.fori_loop(0, pairs // unroll, heads, 0)
     finish()
 
-    @pl.when(jnp.max(bad[...]) > 0.0)
+    @pl.when(jnp.max(r.bad[...]) > 0.0)
     def _():
         def again(pair, _):
             for a in range(subs):
@@ -287,44 +331,45 @@
         finish()
 
 
-def attend(m, states, noise, inner, outer, query, keys, values, w_key, w_value, w_out, w_decode, shares, earlier):
-    members, rows, width = states.shape
-    held = 2 * WIN + rows
-    lanes = w_decode.shape[1]
-    ready = jax.ShapeDtypeStruct((shares, members, rows // shares, lanes), BF)
-    product = jax.ShapeDtypeStruct((width, 2 * lanes), BF)
-    taken = [] if earlier is None else list(earlier)
-
-    def kernel(*refs):
-        ins, rest = refs[:11], refs[11:]
-        if taken:
-            before, w_both, forecast = rest[:3]
-        else:
-            before, w_both, forecast = None, rest[0], rest[1]
-        attend_kernel(m, *ins, before, w_both, forecast, *rest[2 + len(taken) // 2 :])
-
-    return pl.pallas_call(
-        kernel,
-        out_shape=[ready] if taken else [product, ready],
-        in_specs=[VMEM] * (11 + len(taken)),
-        out_specs=[VMEM] * (1 if taken else 2),
-        scratch_shapes=[
-            pltpu.VMEM((2 * WIN, width), BF),
-            pltpu.VMEM((2 * WIN, width), BF),
-            pltpu.VMEM((UNROLL, 2 * held, SUB), BF),
-            pltpu.VMEM((UNROLL, 2 * held, 2 * SUB), BF),
-            pltpu.VMEM((rows, width), BF),
-            pltpu.VMEM((SUB, SUB), F32),
-            pltpu.VMEM((rows, lanes), F32),
-        ],
-        compiler_params=params(24),
+def attend(kind, m, shares, **arrays):
+    members, rows, width = arrays["query"].shape
+    lanes = arrays["base" if kind == "halo" else "w_decode"].shape[1]
+    keep = {"own": rows, "halo": 2 * WIN}.get(kind, 2 * WIN + rows)
+    base = (rows, lanes)
+    unroll = UNROLL[kind]
+    ready = {"forecast": jax.ShapeDtypeStruct((shares, members, rows // shares, lanes), BF)}
+    begun = {
+        "partial": jax.ShapeDtypeStruct((width // SUB, rows, 2 * SUB), F32),
+        "w_both": jax.ShapeDtypeStruct((width, 2 * lanes), BF),
+        "base": jax.ShapeDtypeStruct(base, F32),
+    }
+    scratch = {
+        "kk": pltpu.VMEM((unroll, 2 * keep, SUB), BF),
+        "vv": pltpu.VMEM((unroll, 2 * keep, 2 * SUB), BF),
+    }
+    if kind != "own":
+        scratch["halo_k"] = scratch["halo_v"] = pltpu.VMEM((2 * WIN, width), BF)
+        scratch["mixed"] = pltpu.VMEM((rows, width), BF)
+        scratch["bad"] = pltpu.VMEM((SUB, SUB), F32)
+    if kind == "all":
+        scratch["base"] = pltpu.VMEM(base, F32)
+    outs = begun if kind == "own" else ready
+    names = [*arrays, *outs, *scratch]
+    done = pl.pallas_call(
+        functools.partial(attend_kernel, kind, m, names),
+        out_shape=list(outs.values()),
+        in_specs=[VMEM] * len(arrays),
+        out_specs=[VMEM] * len(outs),
+        scratch_shapes=list(scratch.values()),
+        compiler_params=params(30),
         cost_estimate=pl.CostEstimate(
-            flops=12 * rows * width * width,
+            flops=(12 if kind == "all" else 6) * rows * width * width,
             bytes_accessed=8 * 2**20,
             transcendentals=rows * HEADS * 640,
         ),
-        name="window_attention",
-    )(states, noise, inner, outer, query, keys, values, w_key, w_value, w_out, w_decode, *taken)
+        name="window_" + kind,
+    )(*arrays.values())
+    return dict(zip(outs, done))
 
 
 def crps_kernel(count, gathered, target, grad):
@@ -426,20 +471,21 @@
     chip = [(i, i + 1) for i in range(0, space, 2)]
     both = lambda pairs: pairs + [(j, i) for i, j in pairs]
     far, near, member_noise, w_query = edges(states, member_noise, w_query)
-    outer = [lax.ppermute(far[m], "space", both(cross)) for m in range(members)]
+    outer = lax.ppermute(far, "space", both(cross))
     inner = lax.ppermute(near, "space", both(chip))
     query, keys, values, w_key, w_value = qkv(
         states, member_noise, w_query, w_key, w_value
     )
-    taken = None
-    for m in range(members):
+    own = dict(noise=member_noise, query=query, keys=keys, values=values)
+    halo = dict(inner=inner, outer=outer, w_key=w_key, w_value=w_value)
+    begun = attend("own", 0, ens, states=states, w_out=w_out, w_decode=w_decode, **own)
+    done = attend("halo", 0, ens, **own, **halo, **begun)["forecast"]
+    for m in range(1, members):
         done = attend(
-            m, states, member_noise, inner, outer[m], query, keys, values,
-            w_key, w_value, w_out, w_decode, ens, taken,
-        )
-        product = product if m else done[0]
-        taken = (done[-1], product)
-    gathered = lax.all_to_all(done[-1], "ens", 0, 0)
+            "all", m, ens, states=states, w_decode=w_decode, earlier=done,
+            w_both=begun["w_both"], **own, **halo,
+        )["forecast"]
+    gathered = lax.all_to_all(done, "ens", 0, 0)
     count = members * ens * rows * space * w_decode.shape[1]
     slopes = lax.all_to_all(crps(gathered, target, count), "ens", 0, 0)
     held = slopes.shape[1] - TAIL

time: 141 us -> 139 us (0.986)
  starting transfers between devices: 17 us -> 13.4 us
    ppermute x2 -> x1, starting transfers between devices: 5.59 us -> 3.53 us  [body(): outer = lax.ppermute(far, 'space', both(cross))]
    all_to_all x1, starting transfers between devices: 9.89 us -> 8.34 us  [body(): lax.all_to_all(jnp.broadcast_to(part, (space, 1, part.shape[0])), 'space'...]
    pallas_call x2 -> x3, Pallas kernels: 81.1 us -> 81.3 us  [attend(): pl.pallas_call(functools.partial(attend_kernel, kind, m, names), out_shap...]
  transfers between devices with their start and end apart: 4 -> 3, of which waited for: 1 -> 1; matrix products, arithmetic and copies ran while one was open for 0% -> 0% of each run, Pallas kernels for 36% -> 11%
where the time goes in v4:
time: 139 us
  Pallas kernels  95.3 us (69%)
  blocking collectives  25.4 us (18%)
  starting transfers between devices  13.4 us (10%)
  waiting for transfers between devices  2.95 us (2%)
    pallas_call x3, Pallas kernels, attend(): pl.pallas_call(functools.partial(attend_kernel, kind, m, names), out_shap...  81.3 us
    all_to_all x1, blocking collectives, body(): gathered = lax.all_to_all(done, 'ens', 0, 0)  13.7 us
    all_to_all x1, blocking collectives, body(): slopes = lax.all_to_all(crps(gathered, target, count), 'ens', 0, 0)  11.7 us
    all_to_all x1, starting transfers between devices, body(): lax.all_to_all(jnp.broadcast_to(part, (space, 1, part.shape[0])), 'space'...  8.34 us
    pallas_call x1, Pallas kernels, qkv(): pl.pallas_call(qkv_kernel, out_shape=[jax.ShapeDtypeStruct(states.shape,...  7.45 us
    ppermute x1, starting transfers between devices, body(): outer = lax.ppermute(far, 'space', both(cross))  3.53 us
    all_to_all x1, waiting for transfers between devices, body(): lax.all_to_all(jnp.broadcast_to(part, (space, 1, part.shape[0])), 'space'...  2.94 us
  transfers between devices with their start and end apart: 3, of which 1 were waited for; matrix products, arithmetic and copies ran while one was open for 0% of the time, Pallas kernels for 11%

profile of v4, /device:TPU:1, one launch (start us, length us, event | category | flops | bytes accessed | tf_op | source)
XLA Modules:
  0.0 138.9 jit_solution(7015595070561317931)
XLA Ops:
  0.6 0.0 copy-start
  0.6 2.4 %edges.1 = (bf16[2,256,1024]{2,1,0:T(8,128)(2,1)S(1)}, bf16[2,256,1024]{2,1,0:T(8,128)(2,1)S(1)}, f32[2,1024]{1,0:T(2,128)S(1)}, bf16[1024,1024]{1,0:T(8,128)(2,1)S(1)}) custom-call(bf16[2,512,1024]{2,1,0:T(8,128)(2,1)} %refs_0_.3, f32[2,1024]{1,0:T(2,128)} %noise.1, bf16[1024,1024]{1,0:T(8,128)(2,1)} %w_query.1), custom_call_target="tpu_custom_call" | custom-call | tf_op jit(solution)/shard_map/edges/pallas_call | solution.py:73
  3.1 1.5 %collective-permute-start = (bf16[2,256,1024]{2,1,0:T(8,128)(2,1)S(1)}, bf16[2,256,1024]{2,1,0:T(8,128)(2,1)S(1)}, u32[]{:S(2)}, u32[]{:S(2)}) collective-permute-start(bf16[2,256,1024]{2,1,0:T(8,128)(2,1)S(1)} %get-tuple-element.19), channel_id=1, source_target_pairs={{0,1},{2,3},{4,5},{6,7},{8,9},{10,11},{12,13},{14,15},{1,0},{3,2},... | collective-permute-start | bytes 3145736 | tf_op jit(solution)/shard_map/ppermute | solution.py:475
  4.6 3.5 %collective-permute-start.1 = (bf16[2,256,1024]{2,1,0:T(8,128)(2,1)S(1)}, bf16[2,256,1024]{2,1,0:T(8,128)(2,1)S(1)}, u32[]{:S(2)}, u32[]{:S(2)}) collective-permute-start(bf16[2,256,1024]{2,1,0:T(8,128)(2,1)S(1)} %get-tuple-element.20), channel_id=1, source_target_pairs={{1,2},{3,4},{5,6},{7,8},{9,10},{11,12},{13,14},{2,1},{4,3},{6,5},{... | collective-permute-start | bytes 3145736 | tf_op jit(solution)/shard_map/ppermute | solution.py:474
  8.1 0.0 copy-done
  8.1 0.0 copy-start.2
  8.1 0.0 copy-start.3
  8.1 7.4 %own_qkv.1 = (bf16[2,512,1024]{2,1,0:T(8,128)(2,1)S(1)}, bf16[2,512,1024]{2,1,0:T(8,128)(2,1)S(1)}, bf16[2,512,1024]{2,1,0:T(8,128)(2,1)S(1)}, bf16[1024,1024]{1,0:T(8,128)(2,1)S(1)}, bf16[1024,1024]{1,0:T(8,128)(2,1)S(1)}) custom-call(bf16[2,512,1024]{2,1,0:T(8,128)(2,1)S(1)} %copy-done, f32[2,1024]{1,0:T(2,128)S(1)} %get-tuple-element.14.noise.refs_3_.refs_0_.refs_4_, ...), custom_call_target="tpu_custom_call" | custom-call | flops 6442450944 | bytes 8388608 | tf_op jit(solution)/shard_map/own_qkv/pallas_call | solution.py:118
  15.6 0.0 copy-done.2
  15.6 0.0 copy-done.3
  15.6 5.5 %window_own.1 = (f32[8,512,256]{2,1,0:T(8,128)S(1)}, bf16[1024,256]{1,0:T(8,128)(2,1)S(1)}, f32[512,128]{1,0:T(8,128)S(1)}) custom-call(bf16[2,512,1024]{2,1,0:T(8,128)(2,1)S(1)} %copy-done, bf16[1024,1024]{1,0:T(8,128)(2,1)S(1)} %copy-done.3, bf16[1024,128]{1,0:T(8,128)(2,1)S(1)} %copy-done.2, ...), custom_call_target="tpu_custom_call" | custom-call | flops 3221225472 | bytes 8388608 | tf_op jit(solution)/shard_map/window_own/pallas_call | solution.py:358
  21.1 0.0 collective-permute-done.refs_4_.refs_8_
  21.1 0.0 collective-permute-done.1.refs_5_.refs_9_
  21.1 35.8 %window_halo.1.refs_2_ = bf16[8,2,64,128]{3,2,1,0:T(8,128)(2,1)S(1)} custom-call(f32[2,1024]{1,0:T(2,128)S(1)} %get-tuple-element.14.noise.refs_3_.refs_0_.refs_4_, bf16[2,512,1024]{2,1,0:T(8,128)(2,1)S(1)} %get-tuple-element.16.refs_4_.refs_1_.refs_5_, bf16[2,512,1024]{2,1,0:T(8,128)(2,1)S(1)} %get-tuple-element.17.refs_5_.refs_2_.refs_6_, ...), custom_call_target="tpu_custom_call" | custom-call | flops 3221225472 | bytes 8388608 | tf_op jit(solution)/shard_map/window_halo/pallas_call | solution.py:358
  56.9 0.0 copy-start.1
  56.9 40.1 %window_all.1 = bf16[8,2,64,128]{3,2,1,0:T(8,128)(2,1)S(1)} custom-call(bf16[2,512,1024]{2,1,0:T(8,128)(2,1)S(1)} %copy-done, bf16[1024,128]{1,0:T(8,128)(2,1)S(1)} %copy-done.2, bf16[8,2,64,128]{3,2,1,0:T(8,128)(2,1)S(1)} %window_halo.1.refs_2_, bf16[1024,256]{1,0:T(8,128)(2,1)S(1)} %get-tuple-element.24.refs_9_.refs_3_, ...), custom_call_target="tpu_custom_call" | custom-call | flops 6442450944 | bytes 8388608 | tf_op jit(solution)/shard_map/window_all/pallas_call | solution.py:358
  97.0 13.7 %all_to_all.15.gathered = bf16[8,2,64,128]{3,2,1,0:T(8,128)(2,1)S(1)} all-to-all(bf16[8,2,64,128]{3,2,1,0:T(8,128)(2,1)S(1)} %window_all.1), channel_id=1, replica_groups=mesh['ens'=8,'space'=16] {'ens'}, dimensions={0} | all-to-all | bytes 524288 | tf_op jit(solution)/shard_map/all_to_all | solution.py:488
  110.7 0.0 copy-done.1
  110.8 1.5 %fair_crps.1 = bf16[8,144,128]{2,1,0:T(8,128)(2,1)S(1)} custom-call(bf16[8,2,64,128]{3,2,1,0:T(8,128)(2,1)S(1)} %all_to_all.15.gathered, f32[512,128]{1,0:T(8,128)S(1)} %copy-done.1), custom_call_target="tpu_custom_call" | custom-call | tf_op jit(solution)/shard_map/fair_crps/pallas_call | solution.py:423
  112.2 11.7 %all_to_all.16.slopes = bf16[8,144,128]{2,1,0:T(8,128)(2,1)S(1)} all-to-all(bf16[8,144,128]{2,1,0:T(8,128)(2,1)S(1)} %fair_crps.1), channel_id=1, replica_groups=mesh['ens'=8,'space'=16] {'ens'}, dimensions={0} | all-to-all | bytes 589824 | tf_op jit(solution)/shard_map/all_to_all | solution.py:490
  123.9 0.6 broadcast_in_dim.3
  124.5 8.3 %all-to-all-start.2 = ((f32[16,1,128]{2,1,0:T(1,128)}), f32[16,1,128]{2,1,0:T(1,128)S(1)}, u32[]{:S(2)}, u32[]{:S(2)}) async-start(f32[16,1,128]{2,1,0:T(1,128)} %broadcast_in_dim.3), calls=%async_computation.2 | async-start | bytes 16384 | tf_op jit(solution)/shard_map/all_to_all | solution.py:493
  132.9 2.5 %state_grad.1 = bf16[2,512,1024]{2,1,0:T(8,128)(2,1)} custom-call(bf16[8,144,128]{2,1,0:T(8,128)(2,1)S(1)} %all_to_all.16.slopes, bf16[1024,128]{1,0:T(8,128)(2,1)S(1)} %copy-done.2), custom_call_target="tpu_custom_call" | custom-call | flops 268435456 | bytes 3145728 | tf_op jit(solution)/shard_map/state_grad/pallas_call | solution.py:450
  135.4 2.9 %all-to-all-done.2 = f32[16,1,128]{2,1,0:T(1,128)S(1)} async-done(((f32[16,1,128]{2,1,0:T(1,128)}), f32[16,1,128]{2,1,0:T(1,128)S(1)}, u32[]{:S(2)}, u32[]{:S(2)}) %all-to-all-start.2) | async-done | bytes 8224 | tf_op jit(solution)/shard_map/all_to_all | solution.py:493
  138.3 0.6 reduce_sum.19
  (1 shorter events, 0.0 us)
Async XLA Ops:
  0.6 7.5 %copy-start = (bf16[2,512,1024]{2,1,0:T(8,128)(2,1)S(1)}, bf16[2,512,1024]{2,1,0:T(8,128)(2,1)}, u32[]{:S(2)}) copy-start(bf16[2,512,1024]{2,1,0:T(8,128)(2,1)} %refs_0_.3) | copy-start | bytes 6291460
  3.1 18.0 %collective-permute-start = (bf16[2,256,1024]{2,1,0:T(8,128)(2,1)S(1)}, bf16[2,256,1024]{2,1,0:T(8,128)(2,1)S(1)}, u32[]{:S(2)}, u32[]{:S(2)}) collective-permute-start(bf16[2,256,1024]{2,1,0:T(8,128)(2,1)S(1)} %get-tuple-element.19), channel_id=1, source_target_pairs={{0,1},{2,3},{4,5},{6,7},{8,9},{10,11},{12,13},{14,15},{1,0},{3,2},... | collective-permute-start | bytes 3145736 | tf_op jit(solution)/shard_map/ppermute | solution.py:475
  4.6 16.5 %collective-permute-start.1 = (bf16[2,256,1024]{2,1,0:T(8,128)(2,1)S(1)}, bf16[2,256,1024]{2,1,0:T(8,128)(2,1)S(1)}, u32[]{:S(2)}, u32[]{:S(2)}) collective-permute-start(bf16[2,256,1024]{2,1,0:T(8,128)(2,1)S(1)} %get-tuple-element.20), channel_id=1, source_target_pairs={{1,2},{3,4},{5,6},{7,8},{9,10},{11,12},{13,14},{2,1},{4,3},{6,5},{... | collective-permute-start | bytes 3145736 | tf_op jit(solution)/shard_map/ppermute | solution.py:474
  8.1 7.5 %copy-start.2 = (bf16[1024,128]{1,0:T(8,128)(2,1)S(1)}, bf16[1024,128]{1,0:T(8,128)(2,1)}, u32[]{:S(2)}) copy-start(bf16[1024,128]{1,0:T(8,128)(2,1)} %w_decode.1) | copy-start | bytes 786436
  8.1 7.5 %copy-start.3 = (bf16[1024,1024]{1,0:T(8,128)(2,1)S(1)}, bf16[1024,1024]{1,0:T(8,128)(2,1)}, u32[]{:S(2)}) copy-start(bf16[1024,1024]{1,0:T(8,128)(2,1)} %refs_1_.2) | copy-start | bytes 6291460
  56.9 53.9 %copy-start.1 = (f32[512,128]{1,0:T(8,128)S(1)}, f32[512,128]{1,0:T(8,128)}, u32[]{:S(2)}) copy-start(f32[512,128]{1,0:T(8,128)} %target.1) | copy-start | bytes 786436
  124.5 13.8 %all-to-all-start.2 = ((f32[16,1,128]{2,1,0:T(1,128)}), f32[16,1,128]{2,1,0:T(1,128)S(1)}, u32[]{:S(2)}, u32[]{:S(2)}) async-start(f32[16,1,128]{2,1,0:T(1,128)} %broadcast_in_dim.3), calls=%async_computation.2 | async-start | bytes 16384 | tf_op jit(solution)/shard_map/all_to_all | solution.py:493

commit v5 on v4

--- a/solution.py
+++ b/solution.py
@@ -280,18 +280,17 @@
         return 0
 
     shift = r.noise[m : m + 1]
-    if kind != "halo":
-        constant = jnp.dot(
-            jnp.concatenate([jnp.broadcast_to(x, (8, width)) for x in split(shift, 3)], axis=0),
-            r.w_decode[...],
-            preferred_element_type=F32,
-        )
-        constant = constant[0:1] + constant[8:9] + constant[16:17]
-        r.base[...] = constant + jnp.dot(
-            r.states[m], r.w_decode[...], preferred_element_type=F32
-        )
     if kind == "own":
         lanes = r.w_decode.shape[1]
+        for i in range(members):
+            terms = [jnp.broadcast_to(x, (8, width)) for x in split(r.noise[i : i + 1], 3)]
+            constant = jnp.dot(
+                jnp.concatenate(terms, axis=0), r.w_decode[...], preferred_element_type=F32
+            )
+            constant = constant[0:1] + constant[8:9] + constant[16:17]
+            r.base[i] = constant + jnp.dot(
+                r.states[i], r.w_decode[...], preferred_element_type=F32
+            )
         product = jnp.dot(r.w_out[...], r.w_decode[...], preferred_element_type=F32)
         r.w_both[:, :lanes], r.w_both[:, lanes:] = split(product, 2)
         lax.fori_loop(0, pairs // unroll, heads, 0)
@@ -313,7 +312,7 @@
         for i in range(rows // 256):
             at = slice(i * 256, (i + 1) * 256)
             out = jnp.dot(r.mixed[at], r.w_both[...], preferred_element_type=F32)
-            out = out[:, :lanes] + out[:, lanes:] + r.base[at]
+            out = out[:, :lanes] + out[:, lanes:] + r.base[m, at]
             each = 256 // share
             forecast[i * each : (i + 1) * each, m] = out.astype(BF).reshape(each, share, -1)
 
@@ -333,9 +332,9 @@
 
 def attend(kind, m, shares, **arrays):
     members, rows, width = arrays["query"].shape
-    lanes = arrays["base" if kind == "halo" else "w_decode"].shape[1]
+    lanes = arrays["w_decode" if kind == "own" else "base"].shape[-1]
     keep = {"own": rows, "halo": 2 * WIN}.get(kind, 2 * WIN + rows)
-    base = (rows, lanes)
+    base = (members, rows, lanes)
     unroll = UNROLL[kind]
     ready = {"forecast": jax.ShapeDtypeStruct((shares, members, rows // shares, lanes), BF)}
     begun = {
@@ -351,8 +350,6 @@
         scratch["halo_k"] = scratch["halo_v"] = pltpu.VMEM((2 * WIN, width), BF)
         scratch["mixed"] = pltpu.VMEM((rows, width), BF)
         scratch["bad"] = pltpu.VMEM((SUB, SUB), F32)
-    if kind == "all":
-        scratch["base"] = pltpu.VMEM(base, F32)
     outs = begun if kind == "own" else ready
     names = [*arrays, *outs, *scratch]
     done = pl.pallas_call(
@@ -482,8 +479,7 @@
     done = attend("halo", 0, ens, **own, **halo, **begun)["forecast"]
     for m in range(1, members):
         done = attend(
-            "all", m, ens, states=states, w_decode=w_decode, earlier=done,
-            w_both=begun["w_both"], **own, **halo,
+            "all", m, ens, earlier=done, w_both=begun["w_both"], base=begun["base"], **own, **halo
         )["forecast"]
     gathered = lax.all_to_all(done, "ens", 0, 0)
     count = members * ens * rows * space * w_decode.shape[1]

time: 139 us -> 139 us (level)
  no operation moved by 1% of the time
where the time goes in v5:
time: 139 us
  Pallas kernels  95.4 us (69%)
  blocking collectives  25.4 us (18%)
  starting transfers between devices  13 us (9%)
  waiting for transfers between devices  2.95 us (2%)
    pallas_call x3, Pallas kernels, attend(): pl.pallas_call(functools.partial(attend_kernel, kind, m, names), out_shap...  81.5 us
    all_to_all x1, blocking collectives, body(): gathered = lax.all_to_all(done, 'ens', 0, 0)  13.7 us
    all_to_all x1, blocking collectives, body(): slopes = lax.all_to_all(crps(gathered, target, count), 'ens', 0, 0)  11.7 us
    all_to_all x1, starting transfers between devices, body(): lax.all_to_all(jnp.broadcast_to(part, (space, 1, part.shape[0])), 'space'...  7.94 us
    pallas_call x1, Pallas kernels, qkv(): pl.pallas_call(qkv_kernel, out_shape=[jax.ShapeDtypeStruct(states.shape,...  7.45 us
    ppermute x1, starting transfers between devices, body(): outer = lax.ppermute(far, 'space', both(cross))  3.53 us
    all_to_all x1, waiting for transfers between devices, body(): lax.all_to_all(jnp.broadcast_to(part, (space, 1, part.shape[0])), 'space'...  2.94 us
  transfers between devices with their start and end apart: 3, of which 1 were waited for; matrix products, arithmetic and copies ran while one was open for 0% of the time, Pallas kernels for 11%

profile of v5, /device:TPU:1, one launch (start us, length us, event | category | flops | bytes accessed | tf_op | source)
XLA Modules:
  0.0 138.7 jit_solution(13040044283509047019)
XLA Ops:
  0.6 0.0 copy-start
  0.6 2.4 %edges.1 = (bf16[2,256,1024]{2,1,0:T(8,128)(2,1)S(1)}, bf16[2,256,1024]{2,1,0:T(8,128)(2,1)S(1)}, f32[2,1024]{1,0:T(2,128)S(1)}, bf16[1024,1024]{1,0:T(8,128)(2,1)S(1)}) custom-call(bf16[2,512,1024]{2,1,0:T(8,128)(2,1)} %refs_0_.1, f32[2,1024]{1,0:T(2,128)} %noise.1, bf16[1024,1024]{1,0:T(8,128)(2,1)} %w_query.1), custom_call_target="tpu_custom_call" | custom-call | tf_op jit(solution)/shard_map/edges/pallas_call | solution.py:73
  3.1 1.5 %collective-permute-start = (bf16[2,256,1024]{2,1,0:T(8,128)(2,1)S(1)}, bf16[2,256,1024]{2,1,0:T(8,128)(2,1)S(1)}, u32[]{:S(2)}, u32[]{:S(2)}) collective-permute-start(bf16[2,256,1024]{2,1,0:T(8,128)(2,1)S(1)} %get-tuple-element.19), channel_id=1, source_target_pairs={{0,1},{2,3},{4,5},{6,7},{8,9},{10,11},{12,13},{14,15},{1,0},{3,2},... | collective-permute-start | bytes 3145736 | tf_op jit(solution)/shard_map/ppermute | solution.py:472
  4.6 3.5 %collective-permute-start.1 = (bf16[2,256,1024]{2,1,0:T(8,128)(2,1)S(1)}, bf16[2,256,1024]{2,1,0:T(8,128)(2,1)S(1)}, u32[]{:S(2)}, u32[]{:S(2)}) collective-permute-start(bf16[2,256,1024]{2,1,0:T(8,128)(2,1)S(1)} %get-tuple-element.20), channel_id=1, source_target_pairs={{1,2},{3,4},{5,6},{7,8},{9,10},{11,12},{13,14},{2,1},{4,3},{6,5},{... | collective-permute-start | bytes 3145736 | tf_op jit(solution)/shard_map/ppermute | solution.py:471
  8.1 0.0 copy-done
  8.1 0.0 copy-start.2
  8.1 0.0 copy-start.3
  8.1 7.4 %own_qkv.1 = (bf16[2,512,1024]{2,1,0:T(8,128)(2,1)S(1)}, bf16[2,512,1024]{2,1,0:T(8,128)(2,1)S(1)}, bf16[2,512,1024]{2,1,0:T(8,128)(2,1)S(1)}, bf16[1024,1024]{1,0:T(8,128)(2,1)S(1)}, bf16[1024,1024]{1,0:T(8,128)(2,1)S(1)}) custom-call(bf16[2,512,1024]{2,1,0:T(8,128)(2,1)S(1)} %copy-done, f32[2,1024]{1,0:T(2,128)S(1)} %get-tuple-element.14.noise.refs_3_.refs_0_, ...), custom_call_target="tpu_custom_call" | custom-call | flops 6442450944 | bytes 8388608 | tf_op jit(solution)/shard_map/own_qkv/pallas_call | solution.py:118
  15.6 0.0 copy-done.2
  15.6 0.0 copy-done.3
  15.6 5.9 %window_own.1 = (f32[8,512,256]{2,1,0:T(8,128)S(1)}, bf16[1024,256]{1,0:T(8,128)(2,1)S(1)}, f32[2,512,128]{2,1,0:T(8,128)S(1)}) custom-call(bf16[2,512,1024]{2,1,0:T(8,128)(2,1)S(1)} %copy-done, bf16[1024,1024]{1,0:T(8,128)(2,1)S(1)} %copy-done.3, bf16[1024,128]{1,0:T(8,128)(2,1)S(1)} %copy-done.2, f32[2,1024]{1,0:T(2,128)S(1)} %get-tuple-element.14.noise.refs_3_.refs_0_, ...), custom_call_target="tpu_custom_call" | custom-call | flops 3221225472 | bytes 8388608 | tf_op jit(solution)/shard_map/window_own/pallas_call | solution.py:355
  21.5 0.0 collective-permute-done.refs_4_.refs_7_
  21.5 0.0 collective-permute-done.1.refs_5_.refs_8_
  21.5 35.7 %window_halo.1.refs_0_ = bf16[8,2,64,128]{3,2,1,0:T(8,128)(2,1)S(1)} custom-call(f32[2,1024]{1,0:T(2,128)S(1)} %get-tuple-element.14.noise.refs_3_.refs_0_, bf16[2,512,1024]{2,1,0:T(8,128)(2,1)S(1)} %get-tuple-element.16.refs_4_.refs_1_, bf16[2,512,1024]{2,1,0:T(8,128)(2,1)S(1)} %get-tuple-element.17.refs_5_.refs_2_, ...), custom_call_target="tpu_custom_call" | custom-call | flops 3221225472 | bytes 8388608 | tf_op jit(solution)/shard_map/window_halo/pallas_call | solution.py:355
  57.3 0.0 copy-start.1
  57.3 39.9 %window_all.1 = bf16[8,2,64,128]{3,2,1,0:T(8,128)(2,1)S(1)} custom-call(bf16[8,2,64,128]{3,2,1,0:T(8,128)(2,1)S(1)} %window_halo.1.refs_0_, bf16[1024,256]{1,0:T(8,128)(2,1)S(1)} %get-tuple-element.24.refs_9_.refs_1_, f32[2,512,128]{2,1,0:T(8,128)S(1)} %get-tuple-element.25.refs_10_.refs_2_, f32[2,1024]{1,0:T(2,128)S(1)} %get-tuple-element.14.noise.refs_3_.refs_0_, ...), custom_call_target="tpu_custom_call" | custom-call | flops 6442450944 | bytes 8388608 | tf_op jit(solution)/shard_map/window_all/pallas_call | solution.py:355
  97.2 13.7 %all_to_all.15.gathered = bf16[8,2,64,128]{3,2,1,0:T(8,128)(2,1)S(1)} all-to-all(bf16[8,2,64,128]{3,2,1,0:T(8,128)(2,1)S(1)} %window_all.1), channel_id=1, replica_groups=mesh['ens'=8,'space'=16] {'ens'}, dimensions={0} | all-to-all | bytes 524288 | tf_op jit(solution)/shard_map/all_to_all | solution.py:484
  110.9 0.0 copy-done.1
  110.9 1.5 %fair_crps.1 = bf16[8,144,128]{2,1,0:T(8,128)(2,1)S(1)} custom-call(bf16[8,2,64,128]{3,2,1,0:T(8,128)(2,1)S(1)} %all_to_all.15.gathered, f32[512,128]{1,0:T(8,128)S(1)} %copy-done.1), custom_call_target="tpu_custom_call" | custom-call | tf_op jit(solution)/shard_map/fair_crps/pallas_call | solution.py:420
  112.4 11.7 %all_to_all.16.slopes = bf16[8,144,128]{2,1,0:T(8,128)(2,1)S(1)} all-to-all(bf16[8,144,128]{2,1,0:T(8,128)(2,1)S(1)} %fair_crps.1), channel_id=1, replica_groups=mesh['ens'=8,'space'=16] {'ens'}, dimensions={0} | all-to-all | bytes 589824 | tf_op jit(solution)/shard_map/all_to_all | solution.py:486
  124.1 0.6 broadcast_in_dim.3
  124.7 7.9 %all-to-all-start.2 = ((f32[16,1,128]{2,1,0:T(1,128)}), f32[16,1,128]{2,1,0:T(1,128)S(1)}, u32[]{:S(2)}, u32[]{:S(2)}) async-start(f32[16,1,128]{2,1,0:T(1,128)} %broadcast_in_dim.3), calls=%async_computation.2 | async-start | bytes 16384 | tf_op jit(solution)/shard_map/all_to_all | solution.py:489
  132.7 2.5 %state_grad.1 = bf16[2,512,1024]{2,1,0:T(8,128)(2,1)} custom-call(bf16[8,144,128]{2,1,0:T(8,128)(2,1)S(1)} %all_to_all.16.slopes, bf16[1024,128]{1,0:T(8,128)(2,1)S(1)} %copy-done.2), custom_call_target="tpu_custom_call" | custom-call | flops 268435456 | bytes 3145728 | tf_op jit(solution)/shard_map/state_grad/pallas_call | solution.py:447
  135.2 2.9 %all-to-all-done.2 = f32[16,1,128]{2,1,0:T(1,128)S(1)} async-done(((f32[16,1,128]{2,1,0:T(1,128)}), f32[16,1,128]{2,1,0:T(1,128)S(1)}, u32[]{:S(2)}, u32[]{:S(2)}) %all-to-all-start.2) | async-done | bytes 8224 | tf_op jit(solution)/shard_map/all_to_all | solution.py:489
  138.1 0.6 reduce_sum.19
  (1 shorter events, 0.0 us)
Async XLA Ops:
  0.6 7.5 %copy-start = (bf16[2,512,1024]{2,1,0:T(8,128)(2,1)S(1)}, bf16[2,512,1024]{2,1,0:T(8,128)(2,1)}, u32[]{:S(2)}) copy-start(bf16[2,512,1024]{2,1,0:T(8,128)(2,1)} %refs_0_.1) | copy-start | bytes 6291460
  3.1 18.4 %collective-permute-start = (bf16[2,256,1024]{2,1,0:T(8,128)(2,1)S(1)}, bf16[2,256,1024]{2,1,0:T(8,128)(2,1)S(1)}, u32[]{:S(2)}, u32[]{:S(2)}) collective-permute-start(bf16[2,256,1024]{2,1,0:T(8,128)(2,1)S(1)} %get-tuple-element.19), channel_id=1, source_target_pairs={{0,1},{2,3},{4,5},{6,7},{8,9},{10,11},{12,13},{14,15},{1,0},{3,2},... | collective-permute-start | bytes 3145736 | tf_op jit(solution)/shard_map/ppermute | solution.py:472
  4.6 16.9 %collective-permute-start.1 = (bf16[2,256,1024]{2,1,0:T(8,128)(2,1)S(1)}, bf16[2,256,1024]{2,1,0:T(8,128)(2,1)S(1)}, u32[]{:S(2)}, u32[]{:S(2)}) collective-permute-start(bf16[2,256,1024]{2,1,0:T(8,128)(2,1)S(1)} %get-tuple-element.20), channel_id=1, source_target_pairs={{1,2},{3,4},{5,6},{7,8},{9,10},{11,12},{13,14},{2,1},{4,3},{6,5},{... | collective-permute-start | bytes 3145736 | tf_op jit(solution)/shard_map/ppermute | solution.py:471
  8.1 7.5 %copy-start.2 = (bf16[1024,128]{1,0:T(8,128)(2,1)S(1)}, bf16[1024,128]{1,0:T(8,128)(2,1)}, u32[]{:S(2)}) copy-start(bf16[1024,128]{1,0:T(8,128)(2,1)} %w_decode.1) | copy-start | bytes 786436
  8.1 7.5 %copy-start.3 = (bf16[1024,1024]{1,0:T(8,128)(2,1)S(1)}, bf16[1024,1024]{1,0:T(8,128)(2,1)}, u32[]{:S(2)}) copy-start(bf16[1024,1024]{1,0:T(8,128)(2,1)} %refs_1_.1) | copy-start | bytes 6291460
  57.3 53.7 %copy-start.1 = (f32[512,128]{1,0:T(8,128)S(1)}, f32[512,128]{1,0:T(8,128)}, u32[]{:S(2)}) copy-start(f32[512,128]{1,0:T(8,128)} %target.1) | copy-start | bytes 786436
  124.7 13.4 %all-to-all-start.2 = ((f32[16,1,128]{2,1,0:T(1,128)}), f32[16,1,128]{2,1,0:T(1,128)S(1)}, u32[]{:S(2)}, u32[]{:S(2)}) async-start(f32[16,1,128]{2,1,0:T(1,128)} %broadcast_in_dim.3), calls=%async_computation.2 | async-start | bytes 16384 | tf_op jit(solution)/shard_map/all_to_all | solution.py:489
